TPU v7x, 256 devices: a whole 4x4x8 slice. The times are simulated.
256 devices in a mesh: seq: 32 (over z, x), tensor: 8 (over y, core).
Axes of the slice: x: 4, y: 4, z: 8, core: 2. Of those that a mesh axis runs over, the one named last changes fastest.
Arguments:
- resid: bfloat16 [4096, 4096], P('seq', 'tensor'), may hold values from -40 to 40
- queries: bfloat16 [4096, 4096], P('seq', 'tensor'), may hold values from -8 to 8
- keys: bfloat16 [4096, 4096], P('seq', 'tensor'), may hold values from -6 to 6
- values: bfloat16 [4096, 4096], P('seq', 'tensor'), may hold values from -18 to 18
- doc_ids: int32 [4096], P('seq'), may hold values from 0 to 3, never falling along the last dimension, each value on 1 to 2048 neighbouring positions
- modality: int32 [4096], P('seq'), may hold values from 0 to 2, as said below
- norm_gain: float32 [3, 4096], P(None, 'tensor'), may hold values from 0.1 to 1.9
- gate_w: bfloat16 [4096, 3, 11008], P('tensor', None, 'seq'), may hold values from -0.09375 to 0.09375
- up_w: bfloat16 [4096, 3, 11008], P('tensor', None, 'seq'), may hold values from -0.09375 to 0.09375
- down_weight_matrix: bfloat16 [3, 11008, 4096], P(None, 'seq', 'tensor'), may hold values from -0.0546875 to 0.0546875
Outputs:
- layer_out: bfloat16 [4096, 4096], P('seq', 'tensor')
Inputs may be any that keep to these rules, and one draw needn't show every extreme that they name: `modality`: in each shard of 128 consecutive tokens, at most 48 tokens carry any one tag; in every draw some shard has exactly 48 tokens with tag 0.
All inputs are finite; a program needn't handle non-finite values.
Results may differ from a plain program's by a relative error of at most 0.018.
Values may be sent and summed in bfloat16 or wider, within the bound.
A program may use at most 64 MiB of HBM per device.

v0:
```python
import math

import jax
import jax.numpy as jnp
from jax import lax
from jax.sharding import Mesh
from jax.sharding import PartitionSpec as P

D = 4096
DH = 128
MODS = 3
CAP = 48
SEQ = ("seq_0", "seq_1")


def sent_together(arrays, axis, dim, along):
    widths = [math.prod(a.shape[along:]) for a in arrays]
    both = jnp.concatenate(
        [a.reshape(*a.shape[:along], w) for a, w in zip(arrays, widths)], axis=along
    )
    result = lax.all_gather(both, axis, axis=dim, tiled=True)
    parts = jnp.split(result, [sum(widths[:k]) for k in range(1, len(widths))], axis=along)
    return tuple(
        (b.reshape(*result.shape[:along], *a.shape[along:]) for a, b in zip(arrays, parts))
    )


def sent_to_all(shard, axis):
    devices = lax.axis_size(axis)
    return lax.all_to_all(
        jnp.broadcast_to(shard[None], (devices, *shard.shape)), axis, 0, 0, tiled=True
    )


def taken_together(shard, axis):
    return sent_to_all(shard, axis).sum(axis=0)


def gathered_by_axis(shard, axes, dim):
    for axis in reversed(axes):
        shard = lax.all_gather(shard, axis, axis=dim, tiled=True)
    return shard


def joined_along(parts, dim):
    parts = jnp.moveaxis(parts, 0, dim)
    dims = parts.shape
    return parts.reshape(*dims[:dim], dims[dim] * dims[dim + 1], *dims[dim + 2 :])


def gather_directly(shard, axis, dim):
    parts = sent_to_all(shard, axis)
    return joined_along(parts, dim)


def summed_rows(terms, axes):
    running = terms.astype(jnp.bfloat16)
    for axis in axes:
        running = lax.psum_scatter(running, axis, scatter_dimension=0, tiled=True)
    return running.astype(jnp.float32)


def on_device(
    resid, queries, keys, values, doc_ids, modality, norm_gain, gate_w, up_w, down_weight_matrix
):
    row_count, feat_width = resid.shape
    head_count = feat_width // DH
    seq_count = lax.axis_size(SEQ)
    first_row = lax.axis_index(SEQ) * row_count
    query_pos = first_row + jnp.arange(row_count, dtype=jnp.int32)
    my_docs = doc_ids.astype(jnp.bfloat16)
    query_head_rows = queries.reshape(row_count, head_count, DH)
    scale_factor = 1.0 / math.sqrt(DH)
    key_rows, value_rows, key_docs = sent_together((keys, values, my_docs), SEQ, 0, 1)
    length = key_rows.shape[0]
    key_heads = key_rows.reshape(length, head_count, DH)
    value_heads = value_rows.reshape(length, head_count, DH)
    scores = (
        jnp.einsum("qhd,khd->hqk", query_head_rows, key_heads, preferred_element_type=jnp.float32)
        * scale_factor
    )
    key_pos = jnp.arange(length, dtype=jnp.int32)
    allowed = (key_pos[None, :] <= query_pos[:, None]) & (key_docs[None, :] == my_docs[:, None])
    scores = jnp.where(allowed[None], scores, -1e30)
    old_max = jnp.full((head_count, row_count), -1e30, jnp.float32)
    new_max = jnp.maximum(old_max, jnp.max(scores, axis=2))
    powers = jnp.where(allowed[None], jnp.exp(scores - new_max[:, :, None]), 0.0)
    new_total = jnp.sum(powers, axis=2)
    new_acc = jnp.einsum(
        "hqk,khd->hqd", powers.astype(jnp.bfloat16), value_heads, preferred_element_type=jnp.float32
    )
    attended = (new_acc / new_total[:, :, None]).transpose(1, 0, 2).reshape(row_count, feat_width)
    attended = attended.astype(jnp.bfloat16)
    stream = resid.astype(jnp.float32) + attended.astype(jnp.float32)
    squares = taken_together(jnp.sum(stream * stream, axis=1), "tensor")
    inv_rms = lax.rsqrt(squares / D + 1e-05)
    onehot = (modality[:, None] == jnp.arange(3, dtype=jnp.int32)[None, :]).astype(jnp.float32)
    gain_rows = jnp.dot(onehot, norm_gain, precision=lax.Precision.HIGHEST)
    normalized_input = (stream * inv_rms[:, None] * gain_rows).astype(jnp.bfloat16)
    slot_rank = jnp.sum(onehot * (jnp.cumsum(onehot, axis=0) - 1.0), axis=1)
    slot_grid = jnp.arange(CAP, dtype=jnp.float32)
    placing = onehot.T[:, None, :] * (slot_rank[None, None, :] == slot_grid[None, :, None]).astype(
        jnp.float32
    )
    slot_rows = jnp.einsum(
        "mcr,rf->cmf",
        placing.astype(jnp.bfloat16),
        normalized_input,
        preferred_element_type=jnp.float32,
    ).astype(jnp.bfloat16)
    slot_rows = slot_rows.reshape(CAP, MODS * feat_width)
    unit_count = gate_w.shape[2]
    hidden_cols = MODS * unit_count
    piece = gathered_by_axis(slot_rows, SEQ, 0)
    count = piece.shape[0]
    inputs = piece.reshape(count, MODS, feat_width)
    gate_piece = jnp.einsum("nmd,dmh->nmh", inputs, gate_w, preferred_element_type=jnp.float32)
    up_piece = jnp.einsum("nmd,dmh->nmh", inputs, up_w, preferred_element_type=jnp.float32)
    gate_up = jnp.concatenate(
        [gate_piece.reshape(count, hidden_cols), up_piece.reshape(count, hidden_cols)], axis=1
    )
    summed = lax.psum(gate_up.astype(jnp.bfloat16), "tensor").astype(jnp.float32)
    hidden = (jax.nn.silu(summed[:, :hidden_cols]) * summed[:, hidden_cols:]).astype(jnp.bfloat16)
    every_tag = gather_directly(modality, SEQ, 0)
    tag_grid = every_tag.reshape(seq_count, row_count)
    count = row_count * lax.axis_size(SEQ)
    shard_count = count // row_count
    marks = (tag_grid[:, :, None] == jnp.arange(3, dtype=jnp.int32)[None, None, :]).astype(
        jnp.float32
    )
    ranks = jnp.sum(marks * (jnp.cumsum(marks, axis=1) - 1.0), axis=2)
    spots = marks.transpose(0, 2, 1)[:, :, None, :] * (
        ranks[:, None, None, :] == slot_grid[None, None, :, None]
    ).astype(jnp.float32)
    selected_rows = hidden.reshape(shard_count * CAP, MODS, unit_count)
    slot_part = jnp.einsum(
        "rcu,cuv->rcv", selected_rows, down_weight_matrix, preferred_element_type=jnp.float32
    )
    slot_part = slot_part.reshape(shard_count, CAP, MODS, feat_width)
    placed = jnp.einsum("smcr,scmf->srf", spots, slot_part, precision=lax.Precision.HIGHEST)
    ffn_sum = summed_rows(placed.reshape(count, feat_width), SEQ)
    return (stream + ffn_sum).astype(jnp.bfloat16)


def solution(mesh):
    split = Mesh(mesh.devices.reshape(8, 4, mesh.shape["tensor"]), ("seq_0", "seq_1", "tensor"))
    placed = (
        P(SEQ, "tensor"),
        P(SEQ, "tensor"),
        P(SEQ, "tensor"),
        P(SEQ, "tensor"),
        P(SEQ),
        P(SEQ),
        P(None, "tensor"),
        P("tensor", None, SEQ),
        P("tensor", None, SEQ),
        P(None, SEQ, "tensor"),
    )
    return jax.shard_map(
        on_device, mesh=split, in_specs=placed, out_specs=P(SEQ, "tensor"), check_vma=False
    )
```

profile of v0, /device:TPU:2, one launch (start us, length us, event | category | flops | bytes accessed | tf_op | source)
XLA Modules:
  0.0 421.2 jit_solution(13551106263005902839)
XLA Ops:
  6.5 0.7 fusion.45
  7.3 1.0 copy.56
  8.3 1.0 copy.57
  9.3 0.7 pad_maximum_fusion.1
  10.1 0.0 all-gather.3.cloned.1.call-update
  10.1 0.7 fusion.34
  10.9 0.2 reduce_window_sum.23
  11.0 0.8 select_reduce_fusion.1
  11.9 104.0 %all-gather.3.cloned.1.call-done = bf16[4096,1025]{0,1:T(8,128)(2,1)} async-done(((bf16[128,1025]{0,1:T(8,128)(2,1)}), bf16[4096,1025]{0,1:T(8,128)(2,1)}) %all-gather.3.cloned.1.call-update) | async-done | bytes 8396816 | tf_op jit(solution)/shard_map/all_gather | solution.py:21
  115.9 0.9 slice_reduce_fusion
  116.8 0.7 fusion.14
  117.5 3.8 fusion.44
  121.3 2.4 fusion.2
  123.7 2.1 fusion.4
  125.9 3.2 fusion.26
  129.1 0.1 copy.61
  129.3 0.1 multiply_reduce_fusion
  129.4 0.6 broadcast_in_dim.29
  130.0 4.3 %all-to-all-start.1 = ((f32[8,1,128]{2,1,0:T(1,128)}), f32[8,1,128]{2,1,0:T(1,128)S(1)}, u32[]{:S(2)}, u32[]{:S(2)}) async-start(f32[8,1,128]{2,1,0:T(1,128)} %broadcast_in_dim.29), calls=%async_computation.1 | async-start | bytes 8192 | tf_op jit(solution)/shard_map/all_to_all | solution.py:30
  134.3 0.0 all-gather.5.cloned.1.call-start
  134.4 5.1 %all-to-all-done.1 = f32[8,1,128]{2,1,0:T(1,128)S(1)} async-done(((f32[8,1,128]{2,1,0:T(1,128)}), f32[8,1,128]{2,1,0:T(1,128)S(1)}, u32[]{:S(2)}, u32[]{:S(2)}) %all-to-all-start.1) | async-done | bytes 4128 | tf_op jit(solution)/shard_map/all_to_all | solution.py:30
  139.5 0.3 fusion.22
  139.8 0.2 fusion.21
  140.0 13.7 %all_gather.10 = bf16[192,1536]{1,0:T(8,128)(2,1)} all-gather(bf16[48,1536]{1,0:T(8,128)(2,1)S(1)} %bitcast.82), channel_id=1, replica_groups=mesh['seq_0'=8,'seq_1'=4,'tensor'=8] {'seq_1'}, dimensions={0}, use_global_device_ids=true | all-gather | bytes 737280 | tf_op jit(solution)/shard_map/all_gather | solution.py:41
  153.7 0.0 all-gather.5.cloned.1.call-update
  153.7 0.2 all-reduce.2.cloned.1.call-start
  154.0 57.2 %all-gather.5.cloned.1.call-done = bf16[1536,1536]{1,0:T(8,128)(2,1)} async-done(((bf16[192,1536]{1,0:T(8,128)(2,1)}), bf16[1536,1536]{1,0:T(8,128)(2,1)}) %all-gather.5.cloned.1.call-update) | async-done | bytes 4718608 | tf_op jit(solution)/shard_map/all_gather | solution.py:41
  211.2 6.7 %copy.66 = bf16[1536,1536]{0,1:T(8,128)(2,1)} copy(bf16[1536,1536]{1,0:T(8,128)(2,1)} %all-gather.5.cloned.1.call-done) | data formatting | bytes 9437184 | tf_op jit(solution)/shard_map/all_gather | solution.py:41
  217.9 4.3 %convolution_convert_fusion.1 = bf16[3,1536,344]{1,2,0:T(8,128)(2,1)S(1)} fusion(bf16[1536,3,512]{0,2,1:T(8,128)(2,1)} %bitcast.77, bf16[512,3,344]{0,2,1:T(8,128)(2,1)S(1)} %copy-done.6), kind=kOutput, calls=%fused_computation.14 | convolution fusion | flops 1624780800 | bytes 8945664 | tf_op jit(solution)/shard_map/nmd,dmh->nmh/dot_general | solution.py:117
  222.2 1.8 convolution_convert_fusion
  224.1 3.1 pad_maximum_fusion
  227.1 0.0 all-reduce.2.cloned.1.call-update
  227.2 0.0 reduce-scatter.3.cloned.1.call-start
  227.2 15.8 %all_to_all.12 = s32[32,1,128]{2,1,0:T(1,128)S(1)} all-to-all(s32[32,1,128]{2,1,0:T(1,128)S(1)} %broadcast_in_dim.28), channel_id=1, replica_groups=mesh['seq_0'=8,'seq_1'=4,'tensor'=8] {'seq_0','seq_1'}, dimensions={0} | all-to-all | bytes 32768 | tf_op jit(solution)/shard_map/all_to_all | solution.py:30
  243.0 0.1 copy.62
  243.1 1.7 select_reduce_fusion
  244.8 0.1 copy.63
  244.9 0.1 fusion.30
  245.0 70.8 %all-reduce.2.cloned.1.call-done = bf16[1536,2064]{0,1:T(8,128)(2,1)} async-done(((bf16[1536,2064]{0,1:T(8,128)(2,1)}), bf16[1536,2064]{0,1:T(8,128)(2,1)}) %all-reduce.2.cloned.1.call-update) | async-done | bytes 6340624 | tf_op jit(solution)/shard_map/psum | solution.py:122
  315.8 4.6 %convert_element_type.102 = f32[1536,2064]{0,1:T(8,128)S(1)} convert(bf16[1536,2064]{0,1:T(8,128)(2,1)} %all-reduce.2.cloned.1.call-done) | non-fusion elementwise | flops 3170304 | bytes 19021824 | tf_op jit(solution)/shard_map/convert_element_type | solution.py:122
  320.4 2.1 fusion.3
  322.5 2.6 fusion.46
  325.1 9.7 %bitcast_convert_fusion = bf16[32,128,512]{2,1,0:T(8,128)(2,1)} fusion(f32[32,48,3,512]{3,1,0,2:T(8,128)S(1)} %bitcast.73, f32[32,48,128]{2,1,0:T(8,128)S(1)} %fusion.30, f32[32,3,128]{2,1,0:T(4,128)S(1)} %fusion.35), kind=kOutput, calls=%fused_computation.2 | convolution fusion | flops 3626565632 | bytes 14467072 | tf_op jit(solution)/shard_map/smcr,scmf->srf/dot_general | solution.py:140
  334.9 0.0 reduce-scatter.3.cloned.1.call-update
  334.9 0.0 reduce-scatter.5.cloned.1.call-start
  334.9 55.2 %reduce-scatter.3.cloned.1.call-done = bf16[512,512]{1,0:T(8,128)(2,1)} async-done(((bf16[4096,512]{1,0:T(8,128)(2,1)}), bf16[512,512]{1,0:T(8,128)(2,1)}) %reduce-scatter.3.cloned.1.call-update) | async-done | bytes 524304 | tf_op jit(solution)/shard_map/reduce_scatter | solution.py:59
  390.2 22.9 %reduce-scatter.5.cloned.1.call-done = bf16[128,512]{1,0:T(8,128)(2,1)} async-done(((bf16[512,512]{1,0:T(8,128)(2,1)}), bf16[128,512]{1,0:T(8,128)(2,1)}) %reduce-scatter.5.cloned.1.call-update) | async-done | bytes 131088 | tf_op jit(solution)/shard_map/reduce_scatter | solution.py:59
  413.1 1.6 add_convert_fusion
  (28 shorter events, 0.2 us)
Async XLA Ops:
  6.5 315.9 %copy-start = (bf16[3,344,512]{2,1,0:T(8,128)(2,1)S(1)}, bf16[3,344,512]{2,1,0:T(8,128)(2,1)}, u32[]{:S(2)}) copy-start(bf16[3,344,512]{2,1,0:T(8,128)(2,1)} %param.19) | copy-start | bytes 3170308
  6.5 109.3 %all-gather.3.cloned.1.call-start = ((), (), s32[]{:S(2)}) async-start(), calls=%async_computation.4 | async-start | bytes 8718336 | tf_op jit(solution)/shard_map/all_gather | solution.py:21
  117.5 3.8 copy-start.3
  125.8 3.5 copy-start.2
  125.8 8.5 %copy-start.4 = (s32[128]{0:T(128)S(1)}, s32[128]{0:T(128)}, u32[]{:S(2)}) copy-start(s32[128]{0:T(128)} %param.15) | copy-start | bytes 1540
  125.8 13.7 %copy-start.5 = (f32[3,512]{1,0:T(4,128)S(1)}, f32[3,512]{1,0:T(4,128)}, u32[]{:S(2)}) copy-start(f32[3,512]{1,0:T(4,128)} %param.16) | copy-start | bytes 18436
  130.0 9.5 %all-to-all-start.1 = ((f32[8,1,128]{2,1,0:T(1,128)}), f32[8,1,128]{2,1,0:T(1,128)S(1)}, u32[]{:S(2)}, u32[]{:S(2)}) async-start(f32[8,1,128]{2,1,0:T(1,128)} %broadcast_in_dim.29), calls=%async_computation.1 | async-start | bytes 8192 | tf_op jit(solution)/shard_map/all_to_all | solution.py:30
  134.3 76.9 %all-gather.5.cloned.1.call-start = ((), (), s32[]{:S(2)}) async-start(), calls=%async_computation.5 | async-start | bytes 5308416 | tf_op jit(solution)/shard_map/all_gather | solution.py:41
  153.7 64.2 %copy-start.6 = (bf16[512,3,344]{0,2,1:T(8,128)(2,1)S(1)}, bf16[512,3,344]{0,2,1:T(8,128)(2,1)}, u32[]{:S(2)}) copy-start(bf16[512,3,344]{0,2,1:T(8,128)(2,1)} %param.17) | copy-start | bytes 3170308
  153.7 162.1 %all-reduce.2.cloned.1.call-start = ((), (), s32[]{:S(2)}) async-start(), calls=%async_computation.6 | async-start | bytes 12681216 | tf_op jit(solution)/shard_map/psum | solution.py:122
  217.9 4.3 %copy-start.1 = (bf16[1536,1536]{0,1:T(8,128)(2,1)S(1)}, bf16[1536,1536]{0,1:T(8,128)(2,1)}, u32[]{:S(2)}) copy-start(bf16[1536,1536]{0,1:T(8,128)(2,1)} %copy.66) | copy-start | bytes 14155780
  217.9 4.3 %copy-start.7 = (bf16[512,3,344]{0,2,1:T(8,128)(2,1)S(1)}, bf16[512,3,344]{0,2,1:T(8,128)(2,1)}, u32[]{:S(2)}) copy-start(bf16[512,3,344]{0,2,1:T(8,128)(2,1)} %param.18) | copy-start | bytes 3170308
  227.2 163.0 %reduce-scatter.3.cloned.1.call-start = ((), (), s32[]{:S(2)}) async-start(), calls=%async_computation.7 | async-start | bytes 4718592 | tf_op jit(solution)/shard_map/reduce_scatter | solution.py:59
  334.9 78.2 %reduce-scatter.5.cloned.1.call-start = ((), (), s32[]{:S(2)}) async-start(), calls=%async_computation.8 | async-start | bytes 655360 | tf_op jit(solution)/shard_map/reduce_scatter | solution.py:59
Sparse Core Ops, SparseCore 0:
  10.2 105.5 all-gather.2
  153.8 57.3 all-gather.4
  227.3 88.4 all-reduce.1
  335.0 55.0 reduce-scatter.2
  392.5 20.5 reduce-scatter.4
where the time goes:
time: 424 us; the launch traced here: 421 us
  waiting for transfers between devices  315 us (74%)
  blocking collectives  29.4 us (7%)
  matrix products  24.6 us (6%)
  other arithmetic  19.4 us (5%)
  local copies, waits for them, and re-layouts  14.4 us (3%)
  between operations  13.4 us (3%)
  starting transfers between devices  4.63 us (1%)
    all_gather x1, waiting for transfers between devices, sent_together(): result = lax.all_gather(both, axis, axis=dim, tiled=True)  104 us
    reduce_scatter x2, waiting for transfers between devices, summed_rows(): running = lax.psum_scatter(running, axis, scatter_dimension=0, tiled=True)  78.1 us
    psum x1, waiting for transfers between devices, on_device(): lax.psum(gate_up.astype(jnp.bfloat16), 'tensor').astype(jnp.float32)  70.8 us
    all_gather x1, waiting for transfers between devices, gathered_by_axis(): shard = lax.all_gather(shard, axis, axis=dim, tiled=True)  57.2 us
    all_to_all x1, blocking collectives, sent_to_all(): lax.all_to_all(jnp.broadcast_to(shard[None], (devices, *shard.shape)), ax...  15.8 us
    all_gather x1, blocking collectives, gathered_by_axis(): shard = lax.all_gather(shard, axis, axis=dim, tiled=True)  13.7 us
    dot_general x1, matrix products, on_device(): jnp.einsum('smcr,scmf->srf', spots, slot_part, precision=lax.Precision.HI...  9.73 us
  transfers between devices with their start and end apart: 6, of which 6 were waited for; matrix products, arithmetic and copies ran while one was open for 1% of the time, Pallas kernels for 0%

commit v1 on v0

v1 whole, which is shorter than its diff:
```python
import math

import jax
import jax.numpy as jnp
from jax import lax
from jax.experimental import pallas as pl
from jax.experimental.pallas import tpu as pltpu
from jax.sharding import Mesh
from jax.sharding import PartitionSpec as P

D = 4096
DH = 128
MODS = 3
CAP = 48
ROWS = 128
NZ, NX, NY = 8, 4, 4
BACK = 4
UNITS, WIDE = 344, 384
SEQ = ("z", "x")
TENSOR = ("y", "c")
MESH = pl.DeviceIdType.MESH
F32, BF16 = jnp.float32, jnp.bfloat16


def around(i, by, n):
    return lax.rem(i + (by % n), n)


class Wire:
    def __init__(self, send, recv):
        self.send, self.recv, self.copies = send, recv, []

    def __call__(self, src, dst, to):
        k = len(self.copies)
        copy = pltpu.make_async_remote_copy(
            src_ref=src,
            dst_ref=dst,
            send_sem=self.send.at[k],
            recv_sem=self.recv.at[k],
            device_id=to,
            device_id_type=MESH,
        )
        self.copies.append(copy)
        copy.start()
        return copy

    def drain(self):
        for copy in self.copies:
            copy.wait_send()


def greet(partners):
    barrier = pltpu.get_barrier_semaphore()
    for partner in partners:
        pl.semaphore_signal(barrier, inc=1, device_id=partner, device_id_type=MESH)
    pl.semaphore_wait(barrier, len(partners))


def eye():
    return lax.broadcasted_iota(jnp.int32, (ROWS, ROWS), 0) == lax.broadcasted_iota(
        jnp.int32, (ROWS, ROWS), 1
    )


def to_column(row):
    return jnp.sum(jnp.where(eye(), row, jnp.zeros_like(row)), axis=1, keepdims=True)


def to_row(column):
    return jnp.sum(jnp.where(eye(), column, jnp.zeros_like(column)), axis=0, keepdims=True)


def attend_kernel(
    q_ref, k_ref, v_ref, resid_ref, docs_ref, tags_ref, gain_ref,
    slots_ref, stream_ref,
    qb, kb, vb, db, dcol, top, total, acc, ab, att, sqb, send, recv,
):
    z, x = lax.axis_index("z"), lax.axis_index("x")
    y, c = lax.axis_index("y"), lax.axis_index("c")
    t = 2 * y + c
    tensor_peers = [around(t, o, 8) for o in range(1, 8)]
    tensor_peers = [{"y": p // 2, "c": lax.rem(p, 2)} for p in tensor_peers]
    x_peers = [around(x, o, NX) for o in (1, 3, 2)]
    up, down = {"z": around(z, 1, NZ)}, {"z": around(z, -1, NZ)}
    greet([{"x": p} for p in x_peers] + [up, down] + tensor_peers)
    wire = Wire(send, recv)

    coming = []
    for p in x_peers:
        cols = pl.ds(pl.multiple_of(p * DH, DH), DH)
        coming.append(wire(k_ref.at[:, cols], kb.at[0, x], {"x": p}))
        coming.append(wire(v_ref.at[:, cols], vb.at[0, x], {"x": p}))
        coming.append(wire(docs_ref, db.at[0, x], {"x": p}))
        coming.append(wire(q_ref.at[:, cols], qb.at[x], {"x": p}))
    own = pl.ds(pl.multiple_of(x * DH, DH), DH)
    kb[0, x] = k_ref[:, own]
    vb[0, x] = v_ref[:, own]
    qb[x] = q_ref[:, own]
    db[0, x] = docs_ref[...]
    for copy in coming:
        copy.wait_recv()

    for j in range(NX):
        dcol[j] = to_column(db[0, j])
    scale = 1.0 / math.sqrt(DH)
    for d in range(BACK + 1):
        if d > 0:
            for copy in moving:
                copy.wait_recv()
        if d < BACK:
            moving = [wire(b.at[d], b.at[d + 1], up) for b in (kb, vb, db)]
        first_key = around(z, -d, NZ) * (NX * ROWS)
        keys = kb[d].reshape(NX * ROWS, DH)
        vals = vb[d].reshape(NX * ROWS, DH)
        key_docs = jnp.concatenate([db[d, j] for j in range(NX)], axis=1)

        def block(j, _, d=d, first_key=first_key, keys=keys, vals=vals, key_docs=key_docs):
            score = (
                lax.dot_general(
                    qb[j], keys, (((1,), (1,)), ((), ())), preferred_element_type=F32
                )
                * scale
            )
            query_pos = (z * NX + j) * ROWS + lax.broadcasted_iota(jnp.int32, score.shape, 0)
            key_pos = first_key + lax.broadcasted_iota(jnp.int32, score.shape, 1)
            allowed = (key_pos <= query_pos) & (key_docs == dcol[j])
            score = jnp.where(allowed, score, -1e30)
            high = jnp.max(score, axis=1, keepdims=True)
            if d > 0:
                old = top[j]
                high = jnp.maximum(high, old)
            power = jnp.where(allowed, jnp.exp(score - high), 0.0)
            add = jnp.sum(power, axis=1, keepdims=True)
            blend = jnp.dot(power.astype(BF16), vals, preferred_element_type=F32)
            if d > 0:
                fade = jnp.exp(old - high)
                add = add + fade * total[j]
                blend = blend + fade * acc[j]
            top[j] = high
            total[j] = add
            acc[j] = blend
            if d == BACK:
                ab[j] = (blend / add).astype(BF16)
            return _

        lax.fori_loop(0, NX, block, 0)

    coming = [wire(ab.at[p], att.at[x], {"x": p}) for p in x_peers]
    att[x] = ab[x]
    tag_row = tags_ref[...]
    tag_col = to_column(tag_row)
    for copy in coming:
        copy.wait_recv()
    stream = resid_ref[...].astype(F32) + jnp.concatenate(
        [att[j].astype(F32) for j in range(NX)], axis=1
    )
    stream_ref[...] = stream
    sqb[t] = to_row(jnp.sum(stream * stream, axis=1, keepdims=True))
    coming = [wire(sqb.at[t], sqb.at[t], p) for p in tensor_peers]
    rank = jnp.sum(
        jnp.where(
            (tag_col == tag_row)
            & (
                lax.broadcasted_iota(jnp.int32, (ROWS, ROWS), 0)
                < lax.broadcasted_iota(jnp.int32, (ROWS, ROWS), 1)
            ),
            1.0,
            0.0,
        ),
        axis=0,
        keepdims=True,
    ).astype(jnp.int32)
    slot = lax.broadcasted_iota(jnp.int32, (CAP, ROWS), 0)
    gain = jnp.where(
        tag_col == 0, gain_ref[0:1, :], jnp.where(tag_col == 1, gain_ref[1:2, :], gain_ref[2:3, :])
    )
    scaled = stream
    for copy in coming:
        copy.wait_recv()
    squares = jnp.sum(sqb[...], axis=0)
    inv = to_column(lax.rsqrt(squares / D + 1e-5))
    normed = (scaled * inv * gain).astype(BF16)
    for m in range(MODS):
        placing = jnp.where((tag_row == m) & (rank == slot), 1.0, 0.0).astype(BF16)
        slots_ref[m] = jnp.dot(placing, normed, preferred_element_type=F32).astype(BF16)
    wire.drain()


def gather(wire, axis, n, me, view):
    half = n // 2
    for s in range(1, half + 1):
        last = s == half
        right, left = view(around(me, 1 - s, n), 0 if last else None), view(
            around(me, s - 1, n), 1 if last else None
        )
        moving = [
            wire(right, right, {axis: around(me, 1, n)}),
            wire(left, left, {axis: around(me, -1, n)}),
        ]
        yield
        for copy in moving:
            copy.wait_recv()


def summed(a, b):
    return (a.astype(F32) + b.astype(F32)).astype(BF16)


def scatter(wire, axis, n, me, view, landing, put):
    half = n // 2
    for s in range(1, half + 1):
        far = half - s + 1
        part = (0, 1) if s == 1 else (None, None)
        to = (around(me, far, n), around(me, -far, n))
        if s > 1:
            before = (0, 1) if s == 2 else (None, None)
            for side in (0, 1):
                total = view(to[side], before[side])
                total[...] = summed(total[...], landing(side, s - 1, before[side])[...])
        moving = [
            wire(view(to[side], part[side]), landing(side, s, part[side]), {axis: around(me, by, n)})
            for side, by in ((0, 1), (1, -1))
        ]
        yield
        for copy in moving:
            copy.wait_recv()
    put(
        view(me, None)[...].astype(F32)
        + landing(0, half, None)[...].astype(F32)
        + landing(1, half, None)[...].astype(F32)
    )


def together(*processes):
    active = list(processes)
    while active:
        active = [p for p in active if next(p, "end") != "end"]
        if active:
            yield


def cut(base, part):
    return pl.ds(base, 256) if part is None else pl.ds(base + 128 * part, 128)


def ffn_kernel(
    slots_ref, gate_ref, up_ref, down_ref, stream_ref, tags_ref,
    out_ref,
    xb, pb, cr, ya, yb, hb, yo, za, xa, zc, xc, fin, send, recv,
):
    z, x = lax.axis_index("z"), lax.axis_index("x")
    y, c = lax.axis_index("y"), lax.axis_index("c")
    other = {"c": 1 - c}
    y_right, y_left = {"y": around(y, 1, NY)}, {"y": around(y, -1, NY)}
    greet(
        [{"x": around(x, o, NX)} for o in (1, -1)]
        + [{"z": around(z, o, NZ)} for o in (1, -1)]
        + [y_right, y_left, other]
    )
    wire = Wire(send, recv)
    for m in range(MODS):
        xb[m, z, x] = slots_ref[m]

    def gather_first(m):
        yield from gather(wire, "x", NX, x, lambda j, p: xb.at[m, z, j, :, cut(0, p)])
        yield from gather(wire, "z", NZ, z, lambda j, p: xb.at[m, j, :, :, cut(0, p)])

    def gather_second(m):
        yield from gather(wire, "z", NZ, z, lambda j, p: xb.at[m, j, x, :, cut(256, p)])
        yield from gather(wire, "x", NX, x, lambda j, p: xb.at[m, :, j, :, cut(256, p)])

    def partial(m, plane):
        rows = xb[m, plane].reshape(NX * CAP, 512)
        for k, w_ref in enumerate((gate_ref, up_ref)):
            pb[m, plane, :, k * WIDE : k * WIDE + UNITS] = lax.dot_general(
                rows, w_ref[m], (((1,), (1,)), ((), ())), preferred_element_type=F32
            ).astype(BF16)

    def down_product(m, plane):
        part = jnp.dot(hb[m, plane][:, :UNITS], down_ref[m], preferred_element_type=F32)
        yo[m, plane] = part.astype(BF16).reshape(NX, CAP, 512)

    def middle(m):
        mine = {o: 2 * around(y, o, NY) + c for o in range(NY)}
        theirs = {o: 2 * around(y, o, NY) + 1 - c for o in range(NY)}
        order = (2, 1, 3, 0)
        core = {}
        for o in order:
            partial(m, theirs[o])
            core[o] = wire(pb.at[m, theirs[o]], cr.at[m, o], other)
        yield
        for o in order:
            partial(m, mine[o])
        yield
        for o in order[:3]:
            core[o].wait_recv()
            pb[m, mine[o]] = summed(pb[m, mine[o]], cr[m, o])
            if o == 2:
                moving = [
                    wire(pb.at[m, mine[2], :, pl.ds(0, WIDE)], ya.at[m, 0], y_right),
                    wire(pb.at[m, mine[2], :, pl.ds(WIDE, WIDE)], ya.at[m, 1], y_left),
                ]
        yield
        for copy in moving:
            copy.wait_recv()
        pb[m, mine[1], :, 0:WIDE] = summed(pb[m, mine[1], :, 0:WIDE], ya[m, 0])
        moving = [wire(pb.at[m, mine[1]], yb.at[m, 0], y_right)]
        pb[m, mine[3], :, WIDE:] = summed(pb[m, mine[3], :, WIDE:], ya[m, 1])
        moving.append(wire(pb.at[m, mine[3]], yb.at[m, 1], y_left))
        core[0].wait_recv()
        yield
        for copy in moving:
            copy.wait_recv()
        both = (
            pb[m, mine[0]].astype(F32)
            + cr[m, 0].astype(F32)
            + yb[m, 0].astype(F32)
            + yb[m, 1].astype(F32)
        )
        gate, up = both[:, :WIDE], both[:, WIDE:]
        hb[m, mine[0]] = (gate / (1.0 + jnp.exp(-gate)) * up).astype(BF16)

        def pass_on(plane, to, rows=None):
            ref = hb.at[m, plane] if rows is None else hb.at[m, plane, pl.ds(rows, 96)]
            return wire(ref, ref, to)

        moving = [pass_on(mine[0], y_right), pass_on(mine[0], y_left)]
        across = [pass_on(mine[0], other)]
        down_product(m, mine[0])
        yield
        for copy in moving:
            copy.wait_recv()
        moving = [pass_on(mine[3], y_right, 0), pass_on(mine[1], y_left, 96)]
        across += [pass_on(mine[3], other), pass_on(mine[1], other)]
        down_product(m, mine[3])
        down_product(m, mine[1])
        yield
        for copy in moving:
            copy.wait_recv()
        across.append(pass_on(mine[2], other))
        down_product(m, mine[2])
        for copy, o in zip(across, (0, 3, 1, 2)):
            copy.wait_recv()
            down_product(m, theirs[o])
        yield

    def scatter_first(m):
        def put_z(value):
            yo[m, z, :, :, 0:256] = value.astype(BF16)

        def put(value):
            fin[m, :, 0:256] = value.astype(BF16)

        yield from scatter(
            wire, "z", NZ, z,
            lambda j, p: yo.at[m, j, :, :, cut(0, p)],
            lambda side, s, p: za.at[m, side, s - 1, :, :, cut(0, p)],
            put_z,
        )
        yield from scatter(
            wire, "x", NX, x,
            lambda j, p: yo.at[m, z, j, :, cut(0, p)],
            lambda side, s, p: xa.at[m, side, s - 1, :, cut(0, p)],
            put,
        )

    def scatter_second(m):
        def put_x(value):
            yo[m, :, x, :, 256:512] = value.astype(BF16)

        def put(value):
            fin[m, :, 256:512] = value.astype(BF16)

        yield from scatter(
            wire, "x", NX, x,
            lambda j, p: yo.at[m, :, j, :, cut(256, p)],
            lambda side, s, p: xc.at[m, side, s - 1, :, :, cut(0, p)],
            put_x,
        )
        yield from scatter(
            wire, "z", NZ, z,
            lambda j, p: yo.at[m, j, x, :, cut(256, p)],
            lambda side, s, p: zc.at[m, side, s - 1, :, cut(0, p)],
            put,
        )

    for phase in range(MODS + 2):
        work = []
        if 0 <= phase - 2 < MODS:
            work += [scatter_first(phase - 2), scatter_second(phase - 2)]
        if 0 <= phase - 1 < MODS:
            work.append(middle(phase - 1))
        if phase < MODS:
            work += [gather_first(phase), gather_second(phase)]
        for _ in together(*work):
            pass

    tag_row = tags_ref[...]
    tag_col = to_column(tag_row)
    rank = jnp.sum(
        jnp.where(
            (tag_col == tag_row)
            & (
                lax.broadcasted_iota(jnp.int32, (ROWS, ROWS), 1)
                < lax.broadcasted_iota(jnp.int32, (ROWS, ROWS), 0)
            ),
            1.0,
            0.0,
        ),
        axis=1,
        keepdims=True,
    ).astype(jnp.int32)
    slot = lax.broadcasted_iota(jnp.int32, (ROWS, CAP), 1)
    result = stream_ref[...]
    for m in range(MODS):
        placing = jnp.where((tag_col == m) & (rank == slot), 1.0, 0.0).astype(BF16)
        result = result + jnp.dot(placing, fin[m], preferred_element_type=F32)
    out_ref[...] = result.astype(BF16)
    wire.drain()


def on_device(resid, queries, keys, values, doc_ids, modality, norm_gain, gate_w, up_w, down_w):
    vmem = pl.BlockSpec(memory_space=pltpu.VMEM)
    tags = modality.reshape(1, ROWS)
    block = (NX, ROWS, DH)
    slots, stream = pl.pallas_call(
        attend_kernel,
        out_shape=(
            jax.ShapeDtypeStruct((MODS, CAP, 512), BF16),
            jax.ShapeDtypeStruct((ROWS, 512), F32),
        ),
        in_specs=[vmem] * 7,
        out_specs=(vmem, vmem),
        scratch_shapes=[
            pltpu.VMEM(block, BF16),
            pltpu.VMEM((BACK + 1, *block), BF16),
            pltpu.VMEM((BACK + 1, *block), BF16),
            pltpu.VMEM((BACK + 1, NX, 1, ROWS), jnp.int32),
            pltpu.VMEM((NX, ROWS, 1), jnp.int32),
            pltpu.VMEM((NX, ROWS, 1), F32),
            pltpu.VMEM((NX, ROWS, 1), F32),
            pltpu.VMEM(block, F32),
            pltpu.VMEM(block, BF16),
            pltpu.VMEM(block, BF16),
            pltpu.VMEM((8, 1, ROWS), F32),
            pltpu.SemaphoreType.DMA((40,)),
            pltpu.SemaphoreType.DMA((40,)),
        ],
        compiler_params=pltpu.CompilerParams(
            collective_id=0, has_side_effects=True, vmem_limit_bytes=32 << 20
        ),
        name="attend",
    )(queries, keys, values, resid, doc_ids.reshape(1, ROWS), tags, norm_gain)
    return pl.pallas_call(
        ffn_kernel,
        out_shape=jax.ShapeDtypeStruct((ROWS, 512), BF16),
        in_specs=[vmem] * 6,
        out_specs=vmem,
        scratch_shapes=[
            pltpu.VMEM((MODS, NZ, NX, CAP, 512), BF16),
            pltpu.VMEM((MODS, 8, NX * CAP, 2 * WIDE), BF16),
            pltpu.VMEM((MODS, NY, NX * CAP, 2 * WIDE), BF16),
            pltpu.VMEM((MODS, 2, NX * CAP, WIDE), BF16),
            pltpu.VMEM((MODS, 2, NX * CAP, 2 * WIDE), BF16),
            pltpu.VMEM((MODS, 8, NX * CAP, WIDE), BF16),
            pltpu.VMEM((MODS, NZ, NX, CAP, 512), BF16),
            pltpu.VMEM((MODS, 2, NZ // 2, NX, CAP, 256), BF16),
            pltpu.VMEM((MODS, 2, NX // 2, CAP, 256), BF16),
            pltpu.VMEM((MODS, 2, NZ // 2, CAP, 256), BF16),
            pltpu.VMEM((MODS, 2, NX // 2, NZ, CAP, 256), BF16),
            pltpu.VMEM((MODS, CAP, 512), BF16),
            pltpu.SemaphoreType.DMA((220,)),
            pltpu.SemaphoreType.DMA((220,)),
        ],
        compiler_params=pltpu.CompilerParams(
            collective_id=1, has_side_effects=True, vmem_limit_bytes=60 << 20
        ),
        name="ffn",
    )(
        slots,
        gate_w.transpose(1, 2, 0),
        up_w.transpose(1, 2, 0),
        down_w,
        stream,
        tags,
    )


def solution(mesh):
    split = Mesh(mesh.devices.reshape(NZ, NX, NY, 2), ("z", "x", "y", "c"))
    placed = (
        P(SEQ, TENSOR),
        P(SEQ, TENSOR),
        P(SEQ, TENSOR),
        P(SEQ, TENSOR),
        P(SEQ),
        P(SEQ),
        P(None, TENSOR),
        P(TENSOR, None, SEQ),
        P(TENSOR, None, SEQ),
        P(None, SEQ, TENSOR),
    )
    return jax.shard_map(
        on_device, mesh=split, in_specs=placed, out_specs=P(SEQ, TENSOR), check_vma=False
    )
```

time: 424 us -> 224 us (0.53)
  waiting for transfers between devices: 315 us -> 0 us
  Pallas kernels: 0 us -> 216 us
  blocking collectives: 29.4 us -> 0 us
  matrix products: 24.6 us -> 0 us
  other arithmetic: 19.4 us -> 0 us
  between operations: 13.4 us -> 0.03 us
  local copies, waits for them, and re-layouts: 14.4 us -> 8.54 us
  starting transfers between devices: 4.63 us -> 0 us
    pallas_call x0 -> x2, Pallas kernels: none -> 216 us  [the longest x1 161 us: on_device(): pl.pallas_call(ffn_kernel, out_shape=jax.ShapeDtypeStruct((ROWS, 512), BF...]
    all_gather x2 -> x0, waiting for transfers between devices: 161 us -> none  [the longest x1 104 us: sent_together(): result = lax.all_gather(both, axis, axis=dim, tiled=True)]
    reduce_scatter x2 -> x0, waiting for transfers between devices: 78.1 us -> none  [summed_rows(): running = lax.psum_scatter(running, axis, scatter_dimension=0, tiled=True)]
    psum x1 -> x0, waiting for transfers between devices: 70.8 us -> none  [on_device(): lax.psum(gate_up.astype(jnp.bfloat16), 'tensor').astype(jnp.float32)]
    dot_general x8 -> x0, matrix products: 24.6 us -> none  [the longest x1 9.73 us: on_device(): jnp.einsum('smcr,scmf->srf', spots, slot_part, precision=lax.Precision.HI...]
    all_to_all x1 -> x0, blocking collectives: 15.8 us -> none  [sent_to_all(): lax.all_to_all(jnp.broadcast_to(shard[None], (devices, *shard.shape)), ax...]
    all_gather x1 -> x0, blocking collectives: 13.7 us -> none  [gathered_by_axis(): shard = lax.all_gather(shard, axis, axis=dim, tiled=True)]
    convert_element_type x10 -> x0, other arithmetic: 9.93 us -> none  [the longest x1 4.58 us: on_device(): lax.psum(gate_up.astype(jnp.bfloat16), 'tensor').astype(jnp.float32)]
  transfers between devices with their start and end apart: 6 -> 0, of which waited for: 6 -> 0; matrix products, arithmetic and copies ran while one was open for 1% -> 0% of each run, Pallas kernels for 0% -> 0%
where the time goes in v1:
time: 224 us
  Pallas kernels  216 us (96%)
  local copies, waits for them, and re-layouts  8.54 us (4%)
    pallas_call x1, Pallas kernels, on_device(): pl.pallas_call(ffn_kernel, out_shape=jax.ShapeDtypeStruct((ROWS, 512), BF...  161 us
    pallas_call x1, Pallas kernels, on_device(): pl.pallas_call(attend_kernel, out_shape=(jax.ShapeDtypeStruct((MODS, CAP,...  54.5 us
    unnamed x19, local copies, waits for them, and re-layouts  8.54 us

profile of v1, /device:TPU:2, one launch (start us, length us, event | category | flops | bytes accessed | tf_op | source)
XLA Modules:
  0.0 224.2 jit_solution(70421085707562450)
XLA Ops:
  0.0 0.0 copy-start.2
  0.0 0.9 copy-done.2
  0.9 0.0 copy-start.3
  0.9 0.9 copy-done.3
  1.8 0.0 copy-start.4
  1.8 0.9 copy-done.4
  2.7 0.0 copy-start.5
  2.7 0.9 copy-done.5
  3.6 0.0 copy-start.6
  3.6 0.7 copy-done.6
  4.3 0.0 copy-start.7
  4.3 0.7 copy-done.7
  5.0 0.0 copy-start.8
  5.0 0.7 copy-done.8
  5.6 54.5 %attend.1 = (bf16[3,48,512]{2,1,0:T(8,128)(2,1)S(1)}, f32[128,512]{1,0:T(8,128)S(1)}) custom-call(bf16[128,512]{1,0:T(8,128)(2,1)S(1)} %copy-done.2, bf16[128,512]{1,0:T(8,128)(2,1)S(1)} %copy-done.3, bf16[128,512]{1,0:T(8,128)(2,1)S(1)} %copy-done.4, bf16[128,512]{1,0:T(8,128)(2,1)S(1)} %copy-done.5, s32[1,128]{1,0:T(1,128)S(1)} %bitcast.6, ...), custom_call_target="tpu_custom_call" | custom-call | tf_op jit(solution)/shard_map/attend/pallas_call | solution.py:426
  60.2 0.0 copy-start
  60.2 0.7 copy-done
  60.9 0.0 copy-start.1
  60.9 0.7 copy-done.1
  61.5 161.1 %ffn.1 = bf16[128,512]{1,0:T(8,128)(2,1)} custom-call(bf16[3,48,512]{2,1,0:T(8,128)(2,1)} %copy-done.1, bf16[3,344,512]{2,1,0:T(8,128)(2,1)} %bitcast.7, bf16[3,344,512]{2,1,0:T(8,128)(2,1)} %bitcast.8, bf16[3,344,512]{2,1,0:T(8,128)(2,1)} %down_ref.1, f32[128,512]{1,0:T(8,128)} %copy-done, s32[1,128]{1,0:T(1,128)} %bitcast.4), custom_call_target="tpu_custom_call" | custom-call | tf_op jit(solution)/shard_map/ffn/pallas_call | solution.py:454
  222.6 1.6 copy.12
Async XLA Ops:
  0.0 0.9 copy-start.2
  0.9 0.9 copy-start.3
  1.8 0.9 copy-start.4
  2.7 0.9 copy-start.5
  3.6 0.7 copy-start.6
  4.3 0.7 copy-start.7
  5.0 0.7 copy-start.8
  60.2 0.7 copy-start
  60.9 0.7 copy-start.1

commit v2 on v1

v2 whole, which is shorter than its diff:
```python
import math

import jax
import jax.numpy as jnp
from jax import lax
from jax.experimental import pallas as pl
from jax.experimental.pallas import tpu as pltpu
from jax.sharding import Mesh
from jax.sharding import PartitionSpec as P

D = 4096
DH = 128
MODS = 3
CAP = 48
ROWS = 128
NZ, NX, NY = 8, 4, 4
BACK = 4
TURNED = 3
UNITS, WIDE = 344, 384
HALF = 256
STAGGER = 1
SEQ = ("z", "x")
TENSOR = ("y", "c")
MESH = pl.DeviceIdType.MESH
F32, BF16 = jnp.float32, jnp.bfloat16


def around(i, by, n):
    return lax.rem(i + (by % n), n)


class Wire:
    def __init__(self, send, recv):
        self.send, self.recv, self.copies = send, recv, []

    def __call__(self, src, dst, to):
        k = len(self.copies)
        copy = pltpu.make_async_remote_copy(
            src_ref=src,
            dst_ref=dst,
            send_sem=self.send.at[k],
            recv_sem=self.recv.at[k],
            device_id=to,
            device_id_type=MESH,
        )
        self.copies.append(copy)
        copy.start()
        return copy

    def drain(self):
        for copy in self.copies:
            copy.wait_send()


def landed(copies):
    for copy in copies:
        copy.wait_recv()


def greet(partners):
    barrier = pltpu.get_barrier_semaphore()
    for partner in partners:
        pl.semaphore_signal(barrier, inc=1, device_id=partner, device_id_type=MESH)
    pl.semaphore_wait(barrier, len(partners))


def iota(shape, dim):
    return lax.broadcasted_iota(jnp.int32, shape, dim)


def eye():
    return iota((ROWS, ROWS), 0) == iota((ROWS, ROWS), 1)


def to_column(row):
    return jnp.sum(jnp.where(eye(), row, jnp.zeros_like(row)), axis=1, keepdims=True)


def to_row(column):
    return jnp.sum(jnp.where(eye(), column, jnp.zeros_like(column)), axis=0, keepdims=True)


def attend(wire, here, refs, fetch, xb, stream, scratch):
    z, x, y, c = here
    q_ref, k_ref, v_ref, resid_ref, docs_ref, tags_ref, gain_ref = refs
    qb, kb, vb, kr, vr, db, dcol, top, total, acc, ab, att, sqb, resid, tags, gain = scratch
    t = 2 * y + c
    up, down = {"z": around(z, 1, NZ)}, {"z": around(z, -1, NZ)}
    order = (2, 1, 3, 0)
    at = {o: around(x, o, NX) for o in order}

    def cols(p):
        return pl.ds(pl.multiple_of(p * DH, DH), DH)

    local = [
        fetch(k_ref.at[:, cols(x)], kb.at[0, x]),
        fetch(v_ref.at[:, cols(x)], vb.at[0, x]),
        fetch(docs_ref, db.at[0, x]),
        fetch(q_ref.at[:, cols(x)], qb.at[x]),
        fetch(tags_ref, tags),
        fetch(gain_ref, gain),
        fetch(resid_ref, resid),
    ]
    coming = {"k": [], "v": [], "q": []}
    for o in order[:3]:
        coming["k"].append(wire(k_ref.at[:, cols(at[o])], kb.at[0, x], {"x": at[o]}))
    for o in order[:3]:
        coming["v"].append(wire(v_ref.at[:, cols(at[o])], vb.at[0, x], {"x": at[o]}))
    for o in order[:3]:
        coming["q"].append(wire(docs_ref, db.at[0, x], {"x": at[o]}))
        coming["q"].append(wire(q_ref.at[:, cols(at[o])], qb.at[x], {"x": at[o]}))

    near = pl.ds(0, TURNED)
    rest = pl.ds(TURNED, NX - TURNED)

    def forward(b, r, d):
        if d == BACK:
            return []
        if d + 1 < BACK:
            moving = [wire(b.at[d], b.at[d + 1], up)]
        else:
            moving = [wire(b.at[d, rest], b.at[d + 1, rest], up)]
        source = b.at[0, near] if d == 0 else r.at[d - 1]
        target = b.at[BACK, near] if d + 1 == BACK else r.at[d]
        return moving + [wire(source, target, down)]

    local[0].wait()
    landed(coming["k"])
    moving_k = forward(kb, kr, 0)
    local[1].wait()
    landed(coming["v"])
    moving_v = forward(vb, vr, 0)
    local[2].wait()
    local[3].wait()
    landed(coming["q"])
    moving_d = [wire(db.at[0], db.at[1], up)]
    for o in order:
        dcol[at[o]] = to_column(db[0, at[o]])
    factor = math.log2(math.e) / math.sqrt(DH)
    returned = []

    def block(d, o):
        j = at[o]
        keys = kb[d].reshape(NX * ROWS, DH)
        vals = vb[d].reshape(NX * ROWS, DH)
        key_docs = jnp.concatenate([db[d, i] for i in range(NX)], axis=1)
        score = lax.dot_general(
            qb[j], keys, (((1,), (1,)), ((), ())), preferred_element_type=F32
        )
        if d == 0:
            allowed = (iota(score.shape, 1) <= j * ROWS + iota(score.shape, 0)) & (
                key_docs == dcol[j]
            )
        else:
            allowed = jnp.where(z < d, -1, key_docs) == dcol[j]
        score = jnp.where(allowed, score, -1e30)
        high = jnp.max(score, axis=1, keepdims=True)
        if d > 0:
            old = top[j]
            high = jnp.maximum(high, old)
        power = jnp.exp2((score - high) * factor)
        add = jnp.sum(power, axis=1, keepdims=True)
        blend = jnp.dot(power.astype(BF16), vals, preferred_element_type=F32)
        if d > 0:
            fade = jnp.exp2((old - high) * factor)
            add = add + fade * total[j]
            blend = blend + fade * acc[j]
        if d < BACK:
            top[j] = high
            total[j] = add
            acc[j] = blend
            return
        result = (blend / add).astype(BF16)
        if o == 0:
            att[x] = result
        else:
            ab[j] = result
            returned.append(wire(ab.at[j], att.at[x], {"x": j}))

    for d in range(1, BACK + 1):
        landed(moving_k)
        moving_k = forward(kb, kr, d)
        block(d - 1, 2)
        block(d - 1, 1)
        landed(moving_v)
        moving_v = forward(vb, vr, d)
        landed(moving_d)
        if d < BACK:
            moving_d = [wire(db.at[d], db.at[d + 1], up)]
        block(d - 1, 3)
        block(d - 1, 0)
    for o in order:
        block(BACK, o)

    for copy in local[4:]:
        copy.wait()
    tag_row = tags[...]
    tag_col = to_column(tag_row)
    rank = jnp.sum(
        jnp.where(
            (tag_col == tag_row) & (iota((ROWS, ROWS), 0) < iota((ROWS, ROWS), 1)), 1.0, 0.0
        ),
        axis=0,
        keepdims=True,
    ).astype(jnp.int32)
    slot = iota((CAP, ROWS), 0)
    landed(returned)
    flow = resid[...].astype(F32) + jnp.concatenate(
        [att[i].astype(F32) for i in range(NX)], axis=1
    )
    stream[...] = flow
    sqb[t] = to_row(jnp.sum(flow * flow, axis=1, keepdims=True))
    peers = [around(t, o, 8) for o in range(1, 8)]
    coming = [wire(sqb.at[t], sqb.at[t], {"y": lax.div(p, 2), "c": lax.rem(p, 2)}) for p in peers]
    gains = jnp.where(
        tag_col == 0, gain[0:1, :], jnp.where(tag_col == 1, gain[1:2, :], gain[2:3, :])
    )
    landed(coming)
    inv = to_column(lax.rsqrt(jnp.sum(sqb[...], axis=0) / D + 1e-5))
    normed = (flow * inv * gains).astype(BF16)
    for m in range(MODS):
        placing = jnp.where((tag_row == m) & (rank == slot), 1.0, 0.0).astype(BF16)
        xb[m, lax.div(z, 2), lax.rem(z, 2), x] = jnp.dot(
            placing, normed, preferred_element_type=F32
        ).astype(BF16)


def gather(wire, axis, n, me, view):
    half = n // 2
    for s in range(1, half + 1):
        last = s == half
        right = view(around(me, 1 - s, n), 0 if last else None)
        left = view(around(me, s - 1, n), 1 if last else None)
        moving = [
            wire(right, right, {axis: around(me, 1, n)}),
            wire(left, left, {axis: around(me, -1, n)}),
        ]
        yield
        landed(moving)


def gather_at_once(wire, axis, n, me, view):
    far = sorted(range(1, n), key=lambda o: -min(o, n - o))
    moving = [wire(view(me, None), view(me, None), {axis: around(me, o, n)}) for o in far]
    yield
    landed(moving)


def scatter(wire, axis, n, me, view, landing, put):
    half = n // 2
    for s in range(1, half + 1):
        far = half - s + 1
        part = (0, 1) if s == 1 else (None, None)
        to = (around(me, far, n), around(me, -far, n))
        if s > 1:
            before = (0, 1) if s == 2 else (None, None)
            for side in (0, 1):
                total = view(to[side], before[side])
                total[...] = total[...] + landing(side * half + s - 2, before[side])[...]
        moving = [
            wire(
                view(to[side], part[side]),
                landing(side * half + s - 1, part[side]),
                {axis: around(me, by, n)},
            )
            for side, by in ((0, 1), (1, -1))
        ]
        yield
        landed(moving)
    put(
        view(me, None)[...].astype(F32)
        + landing(half - 1, None)[...].astype(F32)
        + landing(n - 1, None)[...].astype(F32)
    )


def scatter_at_once(wire, axis, n, me, view, landing, put):
    far = sorted(range(1, n), key=lambda o: -min(o, n - o))
    moving = [
        wire(view(around(me, o, n), None), landing(o, None), {axis: around(me, o, n)}) for o in far
    ]
    yield
    landed(moving)
    total = view(me, None)[...].astype(F32)
    for o in range(1, n):
        total = total + landing(o, None)[...].astype(F32)
    put(total)


def together(*processes):
    active = list(processes)
    while active:
        active = [p for p in active if next(p, "end") != "end"]
        if active:
            yield


def cut(base, part):
    return pl.ds(base, HALF) if part is None else pl.ds(base + 128 * part, 128)


def feed_forward(wire, here, weights, xb, scratch):
    z, x, y, c = here
    pb, cr, ya, yb, hb, yo, za, xa, zc, xc, fin = scratch
    gate_w, up_w, down_w, ready = weights
    other = {"c": 1 - c}
    y_right, y_left = {"y": around(y, 1, NY)}, {"y": around(y, -1, NY)}

    def plane(j):
        return lax.div(j, 2), lax.rem(j, 2)

    def gather_first(m):
        yield from gather_at_once(
            wire, "x", NX, x, lambda j, p: xb.at[(m, *plane(z), j, slice(None), cut(0, p))]
        )
        yield from gather(
            wire, "z", NZ, z,
            lambda j, p: xb.at[(m, *plane(j), slice(None), slice(None), cut(0, p))],
        )

    def gather_second(m):
        way = gather_at_once if m == 0 else gather
        yield from way(
            wire, "z", NZ, z, lambda j, p: xb.at[(m, *plane(j), x, slice(None), cut(HALF, p))]
        )
        yield from gather(wire, "x", NX, x, lambda j, p: xb.at[m, :, :, j, :, cut(HALF, p)])

    def partial(m, core, k):
        rows = xb[m, :, core].reshape(NY * NX * CAP, 512)
        value = lax.dot_general(
            rows, (gate_w, up_w)[k][m], (((1,), (1,)), ((), ())), preferred_element_type=F32
        )
        pb[m, :, core, :, k * WIDE : k * WIDE + UNITS] = value.astype(BF16).reshape(
            NY, NX * CAP, UNITS
        )

    def down_product(m, core):
        rows = hb[m, :, core].reshape(NY * NX * CAP, WIDE)[:, :UNITS]
        part = jnp.dot(rows, down_w[m], preferred_element_type=F32)
        yo[m, :, core] = part.astype(BF16).reshape(NY, NX, CAP, 512)

    def middle(m):
        if m == 0:
            ready()
        at = {o: around(y, o, NY) for o in range(NY)}
        core = []
        for k in (0, 1):
            partial(m, 1 - c, k)
            side = pl.ds(k * WIDE, WIDE)
            core.append(wire(pb.at[m, :, 1 - c, :, side], cr.at[m, :, :, side], other))
        yield
        partial(m, c, 0)
        partial(m, c, 1)
        landed(core)
        pb[m, at[2], c] = pb[m, at[2], c] + cr[m, at[2]]
        moving = [
            wire(pb.at[m, at[2], c, :, pl.ds(0, WIDE)], ya.at[m, 0], y_right),
            wire(pb.at[m, at[2], c, :, pl.ds(WIDE, WIDE)], ya.at[m, 1], y_left),
        ]
        for o in (1, 3):
            pb[m, at[o], c] = pb[m, at[o], c] + cr[m, at[o]]
        yield
        landed(moving)
        pb[m, at[1], c, :, 0:WIDE] = pb[m, at[1], c, :, 0:WIDE] + ya[m, 0]
        moving = [wire(pb.at[m, at[1], c], yb.at[m, 0], y_right)]
        pb[m, at[3], c, :, WIDE:] = pb[m, at[3], c, :, WIDE:] + ya[m, 1]
        moving.append(wire(pb.at[m, at[3], c], yb.at[m, 1], y_left))
        yield
        landed(moving)
        both = (
            pb[m, y, c].astype(F32)
            + cr[m, y].astype(F32)
            + yb[m, 0].astype(F32)
            + yb[m, 1].astype(F32)
        )
        gate, up = both[:, :WIDE], both[:, WIDE:]
        hb[m, y, c] = (gate / (1.0 + jnp.exp(-gate)) * up).astype(BF16)

        def pass_on(o, to, rows=None):
            ref = hb.at[m, at[o], c] if rows is None else hb.at[m, at[o], c, pl.ds(rows, 96)]
            return wire(ref, ref, to)

        moving = [pass_on(0, y_right), pass_on(0, y_left)]
        across = [pass_on(0, other)]
        yield
        landed(moving)
        moving = [pass_on(3, y_right, 0), pass_on(1, y_left, 96)]
        across += [pass_on(3, other), pass_on(1, other)]
        yield
        landed(moving)
        across.append(pass_on(2, other))
        down_product(m, c)
        landed(across)
        down_product(m, 1 - c)

    def scatter_first(m):
        def put_z(value):
            yo[(m, *plane(z), slice(None), slice(None), slice(0, HALF))] = value.astype(BF16)

        def put(value):
            fin[m, :, 0:HALF] = value.astype(BF16)

        yield from scatter(
            wire, "z", NZ, z,
            lambda j, p: yo.at[(m, *plane(j), slice(None), slice(None), cut(0, p))],
            lambda k, p: za.at[m, k, :, :, cut(0, p)],
            put_z,
        )
        yield from scatter_at_once(
            wire, "x", NX, x,
            lambda j, p: yo.at[(m, *plane(z), j, slice(None), cut(0, p))],
            lambda k, p: xa.at[m, k, :, cut(0, p)],
            put,
        )

    def scatter_second(m):
        def put_x(value):
            yo[m, :, :, x, :, HALF : 2 * HALF] = value.astype(BF16)

        def put(value):
            fin[m, :, HALF : 2 * HALF] = value.astype(BF16)

        yield from scatter(
            wire, "x", NX, x,
            lambda j, p: yo.at[m, :, :, j, :, cut(HALF, p)],
            lambda k, p: xc.at[m, k, :, :, :, cut(0, p)],
            put_x,
        )
        way = scatter_at_once if m == MODS - 1 else scatter
        yield from way(
            wire, "z", NZ, z,
            lambda j, p: yo.at[(m, *plane(j), x, slice(None), cut(HALF, p))],
            lambda k, p: zc.at[m, k, :, cut(0, p)],
            put,
        )

    def chain(m):
        for _ in range(STAGGER * m):
            yield
        yield from together(gather_first(m), gather_second(m))
        yield from middle(m)
        yield from together(scatter_first(m), scatter_second(m))

    for _ in together(*[chain(m) for m in range(MODS)]):
        pass


def layer_kernel(*args):
    refs, args = args[:7], args[7:]
    (gate_ref, up_ref, down_ref, out_ref), args = args[:4], args[4:]
    (send, recv, local), args = args[:3], args[3:]
    (xb, stream, gate_w, up_w, down_w), args = args[:5], args[5:]
    attend_scratch, ffn_scratch = args[:16], args[16:]
    here = z, x, y, c = tuple(lax.axis_index(a) for a in ("z", "x", "y", "c"))
    peers = [around(2 * y + c, o, 8) for o in range(1, 8)]
    fetched = []

    def fetch(src, dst):
        copy = pltpu.make_async_copy(src, dst, local.at[len(fetched)])
        fetched.append(copy)
        copy.start()
        return copy

    greet(
        [{"x": around(x, o, NX)} for o in range(1, NX)]
        + [{"z": around(z, o, NZ)} for o in range(1, NZ)]
        + [{"y": lax.div(p, 2), "c": lax.rem(p, 2)} for p in peers]
    )
    wire = Wire(send, recv)
    tags, stream_ref, fin = attend_scratch[14], stream, ffn_scratch[-1]
    loads = []

    def ready():
        for copy in loads:
            copy.wait()

    def begin():
        for src, dst in ((gate_ref, gate_w), (up_ref, up_w), (down_ref, down_w)):
            loads.append(fetch(src, dst))

    begin()
    attend(wire, here, refs, fetch, xb, stream_ref, attend_scratch)
    feed_forward(wire, here, (gate_w, up_w, down_w, ready), xb, ffn_scratch)

    tag_row = tags[...]
    tag_col = to_column(tag_row)
    rank = jnp.sum(
        jnp.where(
            (tag_col == tag_row) & (iota((ROWS, ROWS), 1) < iota((ROWS, ROWS), 0)), 1.0, 0.0
        ),
        axis=1,
        keepdims=True,
    ).astype(jnp.int32)
    slot = iota((ROWS, CAP), 1)
    result = stream[...]
    for m in range(MODS):
        placing = jnp.where((tag_col == m) & (rank == slot), 1.0, 0.0).astype(BF16)
        result = result + jnp.dot(placing, fin[m], preferred_element_type=F32)
    out_ref[...] = result.astype(BF16)
    wire.drain()


def on_device(resid, queries, keys, values, doc_ids, modality, norm_gain, gate_w, up_w, down_w):
    block = (NX, ROWS, DH)
    i32 = jnp.int32
    shapes = [
        ((MODS, NY, 2, NX, CAP, 512), BF16),
        ((ROWS, 512), F32),
        ((MODS, UNITS, 512), BF16),
        ((MODS, UNITS, 512), BF16),
        ((MODS, UNITS, 512), BF16),
        (block, BF16),
        ((BACK + 1, *block), BF16),
        ((BACK + 1, *block), BF16),
        ((BACK - 1, TURNED, ROWS, DH), BF16),
        ((BACK - 1, TURNED, ROWS, DH), BF16),
        ((BACK + 1, NX, 1, ROWS), i32),
        ((NX, ROWS, 1), i32),
        ((NX, ROWS, 1), F32),
        ((NX, ROWS, 1), F32),
        (block, F32),
        (block, BF16),
        (block, BF16),
        ((8, 1, ROWS), F32),
        ((ROWS, 512), BF16),
        ((1, ROWS), i32),
        ((MODS, 512), F32),
        ((MODS, NY, 2, NX * CAP, 2 * WIDE), BF16),
        ((MODS, NY, NX * CAP, 2 * WIDE), BF16),
        ((MODS, 2, NX * CAP, WIDE), BF16),
        ((MODS, 2, NX * CAP, 2 * WIDE), BF16),
        ((MODS, NY, 2, NX * CAP, WIDE), BF16),
        ((MODS, NY, 2, NX, CAP, 512), BF16),
        ((MODS, NZ, NX, CAP, HALF), BF16),
        ((MODS, NX, CAP, HALF), BF16),
        ((MODS, NZ, CAP, HALF), BF16),
        ((MODS, NX, NY, 2, CAP, HALF), BF16),
        ((MODS, CAP, 512), BF16),
    ]
    dma = pltpu.SemaphoreType.DMA
    return pl.pallas_call(
        layer_kernel,
        out_shape=jax.ShapeDtypeStruct((ROWS, 512), BF16),
        in_specs=[pl.BlockSpec(memory_space=pl.ANY)] * 10,
        out_specs=pl.BlockSpec(memory_space=pltpu.VMEM),
        scratch_shapes=[dma((280,)), dma((280,)), dma((12,))]
        + [pltpu.VMEM(shape, kind) for shape, kind in shapes],
        compiler_params=pltpu.CompilerParams(
            collective_id=0, has_side_effects=True, vmem_limit_bytes=60 << 20
        ),
        name="layer",
    )(
        queries,
        keys,
        values,
        resid,
        doc_ids.reshape(1, ROWS),
        modality.reshape(1, ROWS),
        norm_gain,
        gate_w.transpose(1, 2, 0),
        up_w.transpose(1, 2, 0),
        down_w,
    )


def solution(mesh):
    split = Mesh(mesh.devices.reshape(NZ, NX, NY, 2), ("z", "x", "y", "c"))
    placed = (
        P(SEQ, TENSOR),
        P(SEQ, TENSOR),
        P(SEQ, TENSOR),
        P(SEQ, TENSOR),
        P(SEQ),
        P(SEQ),
        P(None, TENSOR),
        P(TENSOR, None, SEQ),
        P(TENSOR, None, SEQ),
        P(None, SEQ, TENSOR),
    )
    return jax.shard_map(
        on_device, mesh=split, in_specs=placed, out_specs=P(SEQ, TENSOR), check_vma=False
    )
```

time: 224 us -> 167 us (0.75)
  Pallas kernels: 216 us -> 164 us
  local copies, waits for them, and re-layouts: 8.54 us -> 1.57 us
    pallas_call x2 -> x1, Pallas kernels: 216 us -> 164 us  [on_device(): pl.pallas_call(layer_kernel, out_shape=jax.ShapeDtypeStruct((ROWS, 512),...]
    unnamed x19 -> x1, local copies, waits for them, and re-layouts: 8.54 us -> 1.57 us
where the time goes in v2:
time: 167 us; the launch traced here: 166 us
  Pallas kernels  164 us (98%)
    pallas_call x1, Pallas kernels, on_device(): pl.pallas_call(layer_kernel, out_shape=jax.ShapeDtypeStruct((ROWS, 512),...  164 us

profile of v2, /device:TPU:2, one launch (start us, length us, event | category | flops | bytes accessed | tf_op | source)
XLA Modules:
  0.0 165.6 jit_solution(16035973577259844921)
XLA Ops:
  0.0 164.0 %layer.1 = bf16[128,512]{1,0:T(8,128)(2,1)} custom-call(bf16[128,512]{1,0:T(8,128)(2,1)} %args_0_.4, bf16[128,512]{1,0:T(8,128)(2,1)} %args_1_.4, bf16[128,512]{1,0:T(8,128)(2,1)} %args_2_.4, bf16[128,512]{1,0:T(8,128)(2,1)} %args_3_.4, s32[1,128]{1,0:T(1,128)} %bitcast.6, s32[1,128]{1,0:T(1,128)} %bitcast.7, f32[3,512]{1,0:T(4,128)} %args_6_.4, ...), custom_call_target="tpu_custom_call" | custom-call | tf_op jit(solution)/shard_map/layer/pallas_call | solution.py:541
  164.0 1.6 copy.12

commit v3 on v2

--- a/solution.py
+++ b/solution.py
@@ -18,7 +18,14 @@
 TURNED = 3
 UNITS, WIDE = 344, 384
 HALF = 256
-STAGGER = 1
+PAIR = 2
+WHOLE = 1
+ORDER = (
+    2, 12, 12, 2, 1, 12, 2, 1, 12, 2, 1, 0, 12, 2, 1, 0, 2, 7, 8, 7, 12, 1, 8, 0,
+    1, 7, 12, 6, 5, 0, 8, 6, 5, 7, 0, 8, 6, 0, 3, 5, 4, 7, 3, 4, 8, 6, 5, 7,
+    3, 4, 8, 11, 6, 5, 3, 11, 4, 6, 5, 11, 3, 13, 4, 10, 3, 11, 4, 9, 13, 10, 11, 9,
+    10, 13, 9, 11, 10, 13, 9, 10, 13, 9, 13, 10, 13, 9,
+)
 SEQ = ("z", "x")
 TENSOR = ("y", "c")
 MESH = pl.DeviceIdType.MESH
@@ -80,7 +87,7 @@
     return jnp.sum(jnp.where(eye(), column, jnp.zeros_like(column)), axis=0, keepdims=True)
 
 
-def attend(wire, here, refs, fetch, xb, stream, scratch):
+def attend(wire, here, refs, fetch, lend, xb, xf, stream, scratch):
     z, x, y, c = here
     q_ref, k_ref, v_ref, resid_ref, docs_ref, tags_ref, gain_ref = refs
     qb, kb, vb, kr, vr, db, dcol, top, total, acc, ab, att, sqb, resid, tags, gain = scratch
@@ -109,6 +116,7 @@
     for o in order[:3]:
         coming["q"].append(wire(docs_ref, db.at[0, x], {"x": at[o]}))
         coming["q"].append(wire(q_ref.at[:, cols(at[o])], qb.at[x], {"x": at[o]}))
+    lend()
 
     near = pl.ds(0, TURNED)
     rest = pl.ds(TURNED, NX - TURNED)
@@ -220,9 +228,11 @@
     normed = (flow * inv * gains).astype(BF16)
     for m in range(MODS):
         placing = jnp.where((tag_row == m) & (rank == slot), 1.0, 0.0).astype(BF16)
-        xb[m, lax.div(z, 2), lax.rem(z, 2), x] = jnp.dot(
-            placing, normed, preferred_element_type=F32
-        ).astype(BF16)
+        rows = jnp.dot(placing, normed, preferred_element_type=F32).astype(BF16)
+        if m == WHOLE:
+            xf[lax.div(z, 2), lax.rem(z, 2), x] = rows
+        else:
+            xb[m, lax.div(z, 2), lax.rem(z, 2), lax.div(x, 2)] = rows
 
 
 def gather(wire, axis, n, me, view):
@@ -239,14 +249,7 @@
         landed(moving)
 
 
-def gather_at_once(wire, axis, n, me, view):
-    far = sorted(range(1, n), key=lambda o: -min(o, n - o))
-    moving = [wire(view(me, None), view(me, None), {axis: around(me, o, n)}) for o in far]
-    yield
-    landed(moving)
-
-
-def scatter(wire, axis, n, me, view, landing, put):
+def scatter(wire, axis, n, me, view, landing):
     half = n // 2
     for s in range(1, half + 1):
         far = half - s + 1
@@ -267,189 +270,209 @@
         ]
         yield
         landed(moving)
-    put(
-        view(me, None)[...].astype(F32)
+    total = view(me, None)
+    total[...] = (
+        total[...].astype(F32)
         + landing(half - 1, None)[...].astype(F32)
         + landing(n - 1, None)[...].astype(F32)
-    )
-
-
-def scatter_at_once(wire, axis, n, me, view, landing, put):
-    far = sorted(range(1, n), key=lambda o: -min(o, n - o))
-    moving = [
-        wire(view(around(me, o, n), None), landing(o, None), {axis: around(me, o, n)}) for o in far
-    ]
-    yield
-    landed(moving)
-    total = view(me, None)[...].astype(F32)
-    for o in range(1, n):
-        total = total + landing(o, None)[...].astype(F32)
-    put(total)
-
-
-def together(*processes):
-    active = list(processes)
-    while active:
-        active = [p for p in active if next(p, "end") != "end"]
-        if active:
-            yield
-
-
-def cut(base, part):
+    ).astype(BF16)
+
+
+def cut(part):
+    return pl.ds(0, 512) if part is None else pl.ds(HALF * part, HALF)
+
+
+def side_cut(base, part):
     return pl.ds(base, HALF) if part is None else pl.ds(base + 128 * part, 128)
 
 
-def feed_forward(wire, here, weights, xb, scratch):
+def feed_forward(wire, here, weights, xb, xf, scratch):
     z, x, y, c = here
-    pb, cr, ya, yb, hb, yo, za, xa, zc, xc, fin = scratch
+    pb, cr, ya, yb, hb, yo, za, xa, yf, zf, xs, zs, xf2, fin = scratch
     gate_w, up_w, down_w, ready = weights
+    k = lax.div(x, 2)
+    twin = {"x": around(x, 2, NX)}
     other = {"c": 1 - c}
     y_right, y_left = {"y": around(y, 1, NY)}, {"y": around(y, -1, NY)}
+    rows_of = PAIR * CAP
 
     def plane(j):
         return lax.div(j, 2), lax.rem(j, 2)
 
-    def gather_first(m):
-        yield from gather_at_once(
-            wire, "x", NX, x, lambda j, p: xb.at[(m, *plane(z), j, slice(None), cut(0, p))]
-        )
+    def rows_in(m):
+        mine = xb.at[(m, *plane(z), k)]
+        moving = [wire(mine, mine, twin)]
+        yield
+        landed(moving)
         yield from gather(
             wire, "z", NZ, z,
-            lambda j, p: xb.at[(m, *plane(j), slice(None), slice(None), cut(0, p))],
-        )
-
-    def gather_second(m):
-        way = gather_at_once if m == 0 else gather
-        yield from way(
-            wire, "z", NZ, z, lambda j, p: xb.at[(m, *plane(j), x, slice(None), cut(HALF, p))]
-        )
-        yield from gather(wire, "x", NX, x, lambda j, p: xb.at[m, :, :, j, :, cut(HALF, p)])
-
-    def partial(m, core, k):
-        rows = xb[m, :, core].reshape(NY * NX * CAP, 512)
+            lambda j, p: xb.at[(m, *plane(j), slice(None), slice(None), cut(p))],
+        )
+
+    def whole_first():
+        row = plane(z)
+        mine = xf.at[(*row, x, slice(None), pl.ds(0, HALF))]
+        moving = [wire(mine, mine, {"x": around(x, o, NX)}) for o in (2, 1, 3)]
+        yield
+        landed(moving)
+        yield from gather(
+            wire, "z", NZ, z,
+            lambda j, p: xf.at[(*plane(j), slice(None), slice(None), side_cut(0, p))],
+        )
+
+    def whole_second():
+        yield from gather(
+            wire, "z", NZ, z, lambda j, p: xf.at[(*plane(j), x, slice(None), side_cut(HALF, p))]
+        )
+        yield from gather(wire, "x", NX, x, lambda j, p: xf.at[:, :, j, :, side_cut(HALF, p)])
+
+    def partial(m, e, core, side):
+        if m == WHOLE:
+            rows = xf[:, core, PAIR * e : PAIR * (e + 1)]
+            w = (gate_w, up_w)[side][0, m]
+        else:
+            rows = xb[m, :, core]
+            w = (gate_w, up_w)[side][e, m]
+        rows = rows.reshape(NY * rows_of, 512)
         value = lax.dot_general(
-            rows, (gate_w, up_w)[k][m], (((1,), (1,)), ((), ())), preferred_element_type=F32
-        )
-        pb[m, :, core, :, k * WIDE : k * WIDE + UNITS] = value.astype(BF16).reshape(
-            NY, NX * CAP, UNITS
-        )
-
-    def down_product(m, core):
-        rows = hb[m, :, core].reshape(NY * NX * CAP, WIDE)[:, :UNITS]
-        part = jnp.dot(rows, down_w[m], preferred_element_type=F32)
-        yo[m, :, core] = part.astype(BF16).reshape(NY, NX, CAP, 512)
-
-    def middle(m):
-        if m == 0:
-            ready()
+            rows, w, (((1,), (1,)), ((), ())), preferred_element_type=F32
+        )
+        pb[m, e, :, core, :, side * WIDE : side * WIDE + UNITS] = value.astype(BF16).reshape(
+            NY, rows_of, UNITS
+        )
+
+    def hidden(m, e):
+        ready(m, e)
         at = {o: around(y, o, NY) for o in range(NY)}
         core = []
-        for k in (0, 1):
-            partial(m, 1 - c, k)
-            side = pl.ds(k * WIDE, WIDE)
-            core.append(wire(pb.at[m, :, 1 - c, :, side], cr.at[m, :, :, side], other))
-        yield
-        partial(m, c, 0)
-        partial(m, c, 1)
+        for side in (0, 1):
+            partial(m, e, 1 - c, side)
+            cols = pl.ds(side * WIDE, WIDE)
+            core.append(wire(pb.at[m, e, :, 1 - c, :, cols], cr.at[m, e, :, :, cols], other))
+        yield
+        partial(m, e, c, 0)
+        partial(m, e, c, 1)
         landed(core)
-        pb[m, at[2], c] = pb[m, at[2], c] + cr[m, at[2]]
+        pb[m, e, at[2], c] = pb[m, e, at[2], c] + cr[m, e, at[2]]
         moving = [
-            wire(pb.at[m, at[2], c, :, pl.ds(0, WIDE)], ya.at[m, 0], y_right),
-            wire(pb.at[m, at[2], c, :, pl.ds(WIDE, WIDE)], ya.at[m, 1], y_left),
+            wire(pb.at[m, e, at[2], c, :, pl.ds(0, WIDE)], ya.at[m, e, 0], y_right),
+            wire(pb.at[m, e, at[2], c, :, pl.ds(WIDE, WIDE)], ya.at[m, e, 1], y_left),
         ]
         for o in (1, 3):
-            pb[m, at[o], c] = pb[m, at[o], c] + cr[m, at[o]]
-        yield
-        landed(moving)
-        pb[m, at[1], c, :, 0:WIDE] = pb[m, at[1], c, :, 0:WIDE] + ya[m, 0]
-        moving = [wire(pb.at[m, at[1], c], yb.at[m, 0], y_right)]
-        pb[m, at[3], c, :, WIDE:] = pb[m, at[3], c, :, WIDE:] + ya[m, 1]
-        moving.append(wire(pb.at[m, at[3], c], yb.at[m, 1], y_left))
+            pb[m, e, at[o], c] = pb[m, e, at[o], c] + cr[m, e, at[o]]
+        yield
+        landed(moving)
+        pb[m, e, at[1], c, :, 0:WIDE] = pb[m, e, at[1], c, :, 0:WIDE] + ya[m, e, 0]
+        moving = [wire(pb.at[m, e, at[1], c], yb.at[m, e, 0], y_right)]
+        pb[m, e, at[3], c, :, WIDE:] = pb[m, e, at[3], c, :, WIDE:] + ya[m, e, 1]
+        moving.append(wire(pb.at[m, e, at[3], c], yb.at[m, e, 1], y_left))
         yield
         landed(moving)
         both = (
-            pb[m, y, c].astype(F32)
-            + cr[m, y].astype(F32)
-            + yb[m, 0].astype(F32)
-            + yb[m, 1].astype(F32)
+            pb[m, e, y, c].astype(F32)
+            + cr[m, e, y].astype(F32)
+            + yb[m, e, 0].astype(F32)
+            + yb[m, e, 1].astype(F32)
         )
         gate, up = both[:, :WIDE], both[:, WIDE:]
-        hb[m, y, c] = (gate / (1.0 + jnp.exp(-gate)) * up).astype(BF16)
-
-        def pass_on(o, to, rows=None):
-            ref = hb.at[m, at[o], c] if rows is None else hb.at[m, at[o], c, pl.ds(rows, 96)]
+        hb[m, e, y, c] = (gate / (1.0 + jnp.exp(-gate)) * up).astype(BF16)
+
+        def pass_on(o, to, first=None):
+            ref = hb.at[m, e, at[o], c]
+            if first is not None:
+                ref = hb.at[m, e, at[o], c, pl.ds(first, CAP)]
             return wire(ref, ref, to)
 
         moving = [pass_on(0, y_right), pass_on(0, y_left)]
         across = [pass_on(0, other)]
         yield
         landed(moving)
-        moving = [pass_on(3, y_right, 0), pass_on(1, y_left, 96)]
+        moving = [pass_on(3, y_right, 0), pass_on(1, y_left, CAP)]
         across += [pass_on(3, other), pass_on(1, other)]
         yield
         landed(moving)
         across.append(pass_on(2, other))
-        down_product(m, c)
         landed(across)
-        down_product(m, 1 - c)
-
-    def scatter_first(m):
-        def put_z(value):
-            yo[(m, *plane(z), slice(None), slice(None), slice(0, HALF))] = value.astype(BF16)
-
-        def put(value):
-            fin[m, :, 0:HALF] = value.astype(BF16)
-
+
+    def sums_out(m):
+        for core in (0, 1):
+            part = jnp.zeros((NY * rows_of, 512), F32)
+            for e in (0, 1):
+                rows = hb[m, e, :, core].reshape(NY * rows_of, WIDE)[:, :UNITS]
+                part = part + jnp.dot(rows, down_w[e, m], preferred_element_type=F32)
+            yo[m, :, core] = part.astype(BF16).reshape(NY, PAIR, CAP, 512)
         yield from scatter(
             wire, "z", NZ, z,
-            lambda j, p: yo.at[(m, *plane(j), slice(None), slice(None), cut(0, p))],
-            lambda k, p: za.at[m, k, :, :, cut(0, p)],
-            put_z,
-        )
-        yield from scatter_at_once(
-            wire, "x", NX, x,
-            lambda j, p: yo.at[(m, *plane(z), j, slice(None), cut(0, p))],
-            lambda k, p: xa.at[m, k, :, cut(0, p)],
-            put,
-        )
-
-    def scatter_second(m):
-        def put_x(value):
-            yo[m, :, :, x, :, HALF : 2 * HALF] = value.astype(BF16)
-
-        def put(value):
-            fin[m, :, HALF : 2 * HALF] = value.astype(BF16)
-
+            lambda j, p: yo.at[(m, *plane(j), slice(None), slice(None), cut(p))],
+            lambda n, p: za.at[m, n, :, :, cut(p)],
+        )
+        moving = [wire(yo.at[(m, *plane(z), 1 - k)], xa.at[m], twin)]
+        yield
+        landed(moving)
+        fin[m] = yo[(m, *plane(z), k)] + xa[m]
+
+    made = []
+
+    def products():
+        if made:
+            return
+        made.append(True)
+        for core in (0, 1):
+            for e in (0, 1):
+                rows = hb[WHOLE, e, :, core].reshape(NY * rows_of, WIDE)[:, :UNITS]
+                part = jnp.dot(rows, down_w[0, WHOLE], preferred_element_type=F32)
+                yf[:, core, PAIR * e : PAIR * (e + 1)] = part.astype(BF16).reshape(
+                    NY, PAIR, CAP, 512
+                )
+
+    def whole_out_first():
+        products()
+        yield from scatter(
+            wire, "z", NZ, z,
+            lambda j, p: yf.at[(*plane(j), slice(None), slice(None), side_cut(0, p))],
+            lambda n, p: zf.at[n, :, :, side_cut(0, p)],
+        )
+        moving = []
+        for o in (2, 1, 3):
+            to = around(x, o, NX)
+            source = yf.at[(*plane(z), to, slice(None), pl.ds(0, HALF))]
+            moving.append(wire(source, xs.at[o], {"x": to}))
+        yield
+        landed(moving)
+        total = yf[(*plane(z), x, slice(None), slice(0, HALF))].astype(F32)
+        for o in (1, 2, 3):
+            total = total + xs[o].astype(F32)
+        fin[WHOLE, :, 0:HALF] = total.astype(BF16)
+
+    def whole_out_second():
+        products()
         yield from scatter(
             wire, "x", NX, x,
-            lambda j, p: yo.at[m, :, :, j, :, cut(HALF, p)],
-            lambda k, p: xc.at[m, k, :, :, :, cut(0, p)],
-            put_x,
-        )
-        way = scatter_at_once if m == MODS - 1 else scatter
-        yield from way(
+            lambda j, p: yf.at[:, :, j, :, side_cut(HALF, p)],
+            lambda n, p: xf2.at[n, :, :, :, side_cut(0, p)],
+        )
+        yield from scatter(
             wire, "z", NZ, z,
-            lambda j, p: yo.at[(m, *plane(j), x, slice(None), cut(HALF, p))],
-            lambda k, p: zc.at[m, k, :, cut(0, p)],
-            put,
-        )
-
-    def chain(m):
-        for _ in range(STAGGER * m):
-            yield
-        yield from together(gather_first(m), gather_second(m))
-        yield from middle(m)
-        yield from together(scatter_first(m), scatter_second(m))
-
-    for _ in together(*[chain(m) for m in range(MODS)]):
-        pass
+            lambda j, p: yf.at[(*plane(j), x, slice(None), side_cut(HALF, p))],
+            lambda n, p: zs.at[n, :, side_cut(0, p)],
+        )
+        fin[WHOLE, :, HALF : 2 * HALF] = yf[(*plane(z), x, slice(None), slice(HALF, 2 * HALF))]
+
+    work = [rows_in(0), whole_first(), rows_in(2)]
+    work += [hidden(m, e) for m in range(MODS) for e in (0, 1)]
+    work += [sums_out(0), whole_out_first(), sums_out(2), whole_second(), whole_out_second()]
+    for n in ORDER:
+        next(work[n], None)
+    for process in work:
+        for _ in process:
+            pass
 
 
 def layer_kernel(*args):
     refs, args = args[:7], args[7:]
     (gate_ref, up_ref, down_ref, out_ref), args = args[:4], args[4:]
     (send, recv, local), args = args[:3], args[3:]
-    (xb, stream, gate_w, up_w, down_w), args = args[:5], args[5:]
+    (xb, xf, stream, gate_w, up_w, down_w), args = args[:6], args[6:]
     attend_scratch, ffn_scratch = args[:16], args[16:]
     here = z, x, y, c = tuple(lax.axis_index(a) for a in ("z", "x", "y", "c"))
     peers = [around(2 * y + c, o, 8) for o in range(1, 8)]
@@ -468,19 +491,25 @@
     )
     wire = Wire(send, recv)
     tags, stream_ref, fin = attend_scratch[14], stream, ffn_scratch[-1]
-    loads = []
-
-    def ready():
-        for copy in loads:
-            copy.wait()
-
-    def begin():
-        for src, dst in ((gate_ref, gate_w), (up_ref, up_w), (down_ref, down_w)):
-            loads.append(fetch(src, dst))
-
-    begin()
-    attend(wire, here, refs, fetch, xb, stream_ref, attend_scratch)
-    feed_forward(wire, here, (gate_w, up_w, down_w, ready), xb, ffn_scratch)
+    right, left = {"x": around(x, 1, NX)}, {"x": around(x, -1, NX)}
+    weights = ((gate_ref, gate_w), (up_ref, up_w), (down_ref, down_w))
+    own, lent = [], {}
+
+    def lend():
+        for m in (0, 2):
+            to = left if m == 2 else right
+            lent[m] = [wire(src.at[m], dst.at[1, m], to) for src, dst in weights]
+        for src, dst in weights:
+            own.append(fetch(src, dst.at[0]))
+
+    def ready(m, e):
+        if e == 1 and m != WHOLE:
+            landed(lent[m])
+        while own:
+            own.pop().wait()
+
+    attend(wire, here, refs, fetch, lend, xb, xf, stream_ref, attend_scratch)
+    feed_forward(wire, here, (gate_w, up_w, down_w, ready), xb, xf, ffn_scratch)
 
     tag_row = tags[...]
     tag_col = to_column(tag_row)
@@ -504,11 +533,12 @@
     block = (NX, ROWS, DH)
     i32 = jnp.int32
     shapes = [
-        ((MODS, NY, 2, NX, CAP, 512), BF16),
+        ((MODS, NY, 2, PAIR, CAP, 512), BF16),
+        ((NY, 2, NX, CAP, 512), BF16),
         ((ROWS, 512), F32),
-        ((MODS, UNITS, 512), BF16),
-        ((MODS, UNITS, 512), BF16),
-        ((MODS, UNITS, 512), BF16),
+        ((2, MODS, UNITS, 512), BF16),
+        ((2, MODS, UNITS, 512), BF16),
+        ((2, MODS, UNITS, 512), BF16),
         (block, BF16),
         ((BACK + 1, *block), BF16),
         ((BACK + 1, *block), BF16),
@@ -525,16 +555,19 @@
         ((ROWS, 512), BF16),
         ((1, ROWS), i32),
         ((MODS, 512), F32),
-        ((MODS, NY, 2, NX * CAP, 2 * WIDE), BF16),
-        ((MODS, NY, NX * CAP, 2 * WIDE), BF16),
-        ((MODS, 2, NX * CAP, WIDE), BF16),
-        ((MODS, 2, NX * CAP, 2 * WIDE), BF16),
-        ((MODS, NY, 2, NX * CAP, WIDE), BF16),
-        ((MODS, NY, 2, NX, CAP, 512), BF16),
-        ((MODS, NZ, NX, CAP, HALF), BF16),
-        ((MODS, NX, CAP, HALF), BF16),
-        ((MODS, NZ, CAP, HALF), BF16),
-        ((MODS, NX, NY, 2, CAP, HALF), BF16),
+        ((MODS, 2, NY, 2, PAIR * CAP, 2 * WIDE), BF16),
+        ((MODS, 2, NY, PAIR * CAP, 2 * WIDE), BF16),
+        ((MODS, 2, 2, PAIR * CAP, WIDE), BF16),
+        ((MODS, 2, 2, PAIR * CAP, 2 * WIDE), BF16),
+        ((MODS, 2, NY, 2, PAIR * CAP, WIDE), BF16),
+        ((MODS, NY, 2, PAIR, CAP, 512), BF16),
+        ((MODS, NZ, PAIR, CAP, 512), BF16),
+        ((MODS, CAP, 512), BF16),
+        ((NY, 2, NX, CAP, 512), BF16),
+        ((NZ, NX, CAP, HALF), BF16),
+        ((NX, CAP, HALF), BF16),
+        ((NZ, CAP, HALF), BF16),
+        ((NX, NY, 2, CAP, HALF), BF16),
         ((MODS, CAP, 512), BF16),
     ]
     dma = pltpu.SemaphoreType.DMA

time: 167 us -> 152 us (0.910)
  Pallas kernels: 164 us -> 150 us
    pallas_call x1, Pallas kernels: 164 us -> 150 us  [on_device(): pl.pallas_call(layer_kernel, out_shape=jax.ShapeDtypeStruct((ROWS, 512),...]
where the time goes in v3:
time: 152 us; the launch traced here: 151 us
  Pallas kernels  150 us (99%)
  local copies, waits for them, and re-layouts  1.57 us (1%)
    pallas_call x1, Pallas kernels, on_device(): pl.pallas_call(layer_kernel, out_shape=jax.ShapeDtypeStruct((ROWS, 512),...  150 us

profile of v3, /device:TPU:2, one launch (start us, length us, event | category | flops | bytes accessed | tf_op | source)
XLA Modules:
  0.0 151.1 jit_solution(5983486375557564221)
XLA Ops:
  0.0 149.5 %layer.1 = bf16[128,512]{1,0:T(8,128)(2,1)} custom-call(bf16[128,512]{1,0:T(8,128)(2,1)} %args_0_.4, bf16[128,512]{1,0:T(8,128)(2,1)} %args_1_.4, bf16[128,512]{1,0:T(8,128)(2,1)} %args_2_.4, bf16[128,512]{1,0:T(8,128)(2,1)} %args_3_.4, s32[1,128]{1,0:T(1,128)} %bitcast.6, s32[1,128]{1,0:T(1,128)} %bitcast.7, f32[3,512]{1,0:T(4,128)} %args_6_.4, ...), custom_call_target="tpu_custom_call" | custom-call | tf_op jit(solution)/shard_map/layer/pallas_call | solution.py:574
  149.5 1.6 %copy.12 = bf16[128,512]{1,0:T(8,128)(2,1)} copy(bf16[128,512]{1,0:T(8,128)(2,1)} %layer.1) | data formatting | bytes 262144

commit v4 on v3

--- a/solution.py
+++ b/solution.py
@@ -21,10 +21,11 @@
 PAIR = 2
 WHOLE = 1
 ORDER = (
-    2, 12, 12, 2, 1, 12, 2, 1, 12, 2, 1, 0, 12, 2, 1, 0, 2, 7, 8, 7, 12, 1, 8, 0,
-    1, 7, 12, 6, 5, 0, 8, 6, 5, 7, 0, 8, 6, 0, 3, 5, 4, 7, 3, 4, 8, 6, 5, 7,
-    3, 4, 8, 11, 6, 5, 3, 11, 4, 6, 5, 11, 3, 13, 4, 10, 3, 11, 4, 9, 13, 10, 11, 9,
-    10, 13, 9, 11, 10, 13, 9, 10, 13, 9, 13, 10, 13, 9,
+    15, 2, 12, 15, 12, 2, 15, 12, 2, 1, 15, 12, 2, 15, 12, 1, 2, 14, 1, 2, 0, 15, 7, 8,
+    14, 7, 8, 1, 12, 0, 14, 7, 8, 1, 12, 0, 14, 7, 1, 5, 6, 0, 14, 8, 5, 7, 6, 0,
+    8, 5, 0, 7, 14, 4, 6, 8, 17, 5, 11, 4, 3, 6, 11, 5, 3, 4, 17, 11, 6, 5, 3, 17,
+    11, 4, 17, 6, 10, 11, 17, 3, 13, 4, 10, 11, 17, 3, 13, 4, 10, 3, 16, 9, 13, 10, 9, 13,
+    10, 16, 9, 13, 16, 10, 9, 13, 16, 9, 13, 16, 9, 16,
 )
 SEQ = ("z", "x")
 TENSOR = ("y", "c")
@@ -108,97 +109,96 @@
         fetch(gain_ref, gain),
         fetch(resid_ref, resid),
     ]
-    coming = {"k": [], "v": [], "q": []}
+    sides = ((k_ref, kb, kr), (v_ref, vb, vr))
+    coming, asked = {}, []
     for o in order[:3]:
-        coming["k"].append(wire(k_ref.at[:, cols(at[o])], kb.at[0, x], {"x": at[o]}))
+        coming[o] = [wire(ref.at[:, cols(at[o])], b.at[0, x], {"x": at[o]}) for ref, b, _ in sides]
+    slot = {o: around(x, -o, NX) for o in order}
+    rising = {0: [wire(ref.at[:, cols(x)], b.at[1, x], up) for ref, b, _ in sides]}
+    falling = {}
     for o in order[:3]:
-        coming["v"].append(wire(v_ref.at[:, cols(at[o])], vb.at[0, x], {"x": at[o]}))
+        asked.append(wire(docs_ref, db.at[0, x], {"x": at[o]}))
+        asked.append(wire(q_ref.at[:, cols(at[o])], qb.at[x], {"x": at[o]}))
+    lend()
+
     for o in order[:3]:
-        coming["q"].append(wire(docs_ref, db.at[0, x], {"x": at[o]}))
-        coming["q"].append(wire(q_ref.at[:, cols(at[o])], qb.at[x], {"x": at[o]}))
-    lend()
-
-    near = pl.ds(0, TURNED)
-    rest = pl.ds(TURNED, NX - TURNED)
-
-    def forward(b, r, d):
+        rising[o], falling[o] = [], []
+        for copy, (_, b, r) in zip(coming[o], sides):
+            copy.wait_recv()
+            rising[o].append(wire(b.at[0, slot[o]], b.at[1, slot[o]], up))
+            falling[o].append(wire(b.at[0, slot[o]], r.at[0, o - 1], down))
+
+    def pass_on(d, o):
+        came, fell = rising.pop(o, []), falling.pop(o, [])
+        landed(came + fell)
         if d == BACK:
-            return []
-        if d + 1 < BACK:
-            moving = [wire(b.at[d], b.at[d + 1], up)]
-        else:
-            moving = [wire(b.at[d, rest], b.at[d + 1, rest], up)]
-        source = b.at[0, near] if d == 0 else r.at[d - 1]
-        target = b.at[BACK, near] if d + 1 == BACK else r.at[d]
-        return moving + [wire(source, target, down)]
+            return
+        rising[o], falling[o] = [], []
+        for _, b, r in sides:
+            if d + 1 < BACK or o == 0:
+                rising[o].append(wire(b.at[d, slot[o]], b.at[d + 1, slot[o]], up))
+            if o > 0:
+                target = b.at[BACK, slot[o]] if d + 1 == BACK else r.at[d, o - 1]
+                falling[o].append(wire(r.at[d - 1, o - 1], target, down))
 
     local[0].wait()
-    landed(coming["k"])
-    moving_k = forward(kb, kr, 0)
     local[1].wait()
-    landed(coming["v"])
-    moving_v = forward(vb, vr, 0)
     local[2].wait()
     local[3].wait()
-    landed(coming["q"])
+    landed(asked)
     moving_d = [wire(db.at[0], db.at[1], up)]
     for o in order:
         dcol[at[o]] = to_column(db[0, at[o]])
     factor = math.log2(math.e) / math.sqrt(DH)
     returned = []
 
-    def block(d, o):
-        j = at[o]
+    def block(d, j, n):
+        some, rows = pl.ds(j, n), n * ROWS
         keys = kb[d].reshape(NX * ROWS, DH)
         vals = vb[d].reshape(NX * ROWS, DH)
         key_docs = jnp.concatenate([db[d, i] for i in range(NX)], axis=1)
         score = lax.dot_general(
-            qb[j], keys, (((1,), (1,)), ((), ())), preferred_element_type=F32
+            qb[some].reshape(rows, DH), keys, (((1,), (1,)), ((), ())), preferred_element_type=F32
         )
         if d == 0:
             allowed = (iota(score.shape, 1) <= j * ROWS + iota(score.shape, 0)) & (
-                key_docs == dcol[j]
+                key_docs == dcol[some].reshape(rows, 1)
             )
         else:
-            allowed = jnp.where(z < d, -1, key_docs) == dcol[j]
+            allowed = jnp.where(z < d, -1, key_docs) == dcol[some].reshape(rows, 1)
         score = jnp.where(allowed, score, -1e30)
         high = jnp.max(score, axis=1, keepdims=True)
         if d > 0:
-            old = top[j]
+            old = top[some].reshape(rows, 1)
             high = jnp.maximum(high, old)
         power = jnp.exp2((score - high) * factor)
         add = jnp.sum(power, axis=1, keepdims=True)
         blend = jnp.dot(power.astype(BF16), vals, preferred_element_type=F32)
         if d > 0:
             fade = jnp.exp2((old - high) * factor)
-            add = add + fade * total[j]
-            blend = blend + fade * acc[j]
+            add = add + fade * total[some].reshape(rows, 1)
+            blend = blend + fade * acc[some].reshape(rows, DH)
         if d < BACK:
-            top[j] = high
-            total[j] = add
-            acc[j] = blend
-            return
-        result = (blend / add).astype(BF16)
-        if o == 0:
-            att[x] = result
-        else:
-            ab[j] = result
-            returned.append(wire(ab.at[j], att.at[x], {"x": j}))
+            top[some] = high.reshape(n, ROWS, 1)
+            total[some] = add.reshape(n, ROWS, 1)
+            acc[some] = blend.reshape(n, ROWS, DH)
+            return None
+        return (blend / add).astype(BF16)
 
     for d in range(1, BACK + 1):
-        landed(moving_k)
-        moving_k = forward(kb, kr, d)
-        block(d - 1, 2)
-        block(d - 1, 1)
-        landed(moving_v)
-        moving_v = forward(vb, vr, d)
+        pass_on(d, 0)
+        pass_on(d, 2)
+        block(d - 1, 0, 2)
+        pass_on(d, 1)
+        pass_on(d, 3)
         landed(moving_d)
         if d < BACK:
             moving_d = [wire(db.at[d], db.at[d + 1], up)]
-        block(d - 1, 3)
-        block(d - 1, 0)
-    for o in order:
-        block(BACK, o)
+        block(d - 1, 2, 2)
+    for o in order[:3]:
+        ab[at[o]] = block(BACK, at[o], 1)
+        returned.append(wire(ab.at[at[o]], att.at[x], {"x": at[o]}))
+    att[x] = block(BACK, x, 1)
 
     for copy in local[4:]:
         copy.wait()
@@ -211,7 +211,7 @@
         axis=0,
         keepdims=True,
     ).astype(jnp.int32)
-    slot = iota((CAP, ROWS), 0)
+    place = iota((CAP, ROWS), 0)
     landed(returned)
     flow = resid[...].astype(F32) + jnp.concatenate(
         [att[i].astype(F32) for i in range(NX)], axis=1
@@ -227,7 +227,7 @@
     inv = to_column(lax.rsqrt(jnp.sum(sqb[...], axis=0) / D + 1e-5))
     normed = (flow * inv * gains).astype(BF16)
     for m in range(MODS):
-        placing = jnp.where((tag_row == m) & (rank == slot), 1.0, 0.0).astype(BF16)
+        placing = jnp.where((tag_row == m) & (rank == place), 1.0, 0.0).astype(BF16)
         rows = jnp.dot(placing, normed, preferred_element_type=F32).astype(BF16)
         if m == WHOLE:
             xf[lax.div(z, 2), lax.rem(z, 2), x] = rows
@@ -278,17 +278,13 @@
     ).astype(BF16)
 
 
-def cut(part):
-    return pl.ds(0, 512) if part is None else pl.ds(HALF * part, HALF)
-
-
 def side_cut(base, part):
     return pl.ds(base, HALF) if part is None else pl.ds(base + 128 * part, 128)
 
 
 def feed_forward(wire, here, weights, xb, xf, scratch):
     z, x, y, c = here
-    pb, cr, ya, yb, hb, yo, za, xa, yf, zf, xs, zs, xf2, fin = scratch
+    pb, cr, ya, yb, hb, yo, za, xa, zt, xt, yf, zf, xs, zs, xf2, fin = scratch
     gate_w, up_w, down_w, ready = weights
     k = lax.div(x, 2)
     twin = {"x": around(x, 2, NX)}
@@ -299,15 +295,25 @@
     def plane(j):
         return lax.div(j, 2), lax.rem(j, 2)
 
-    def rows_in(m):
-        mine = xb.at[(m, *plane(z), k)]
+    def rows_first(m):
+        mine = xb.at[(m, *plane(z), k, slice(None), pl.ds(0, HALF))]
         moving = [wire(mine, mine, twin)]
         yield
         landed(moving)
         yield from gather(
             wire, "z", NZ, z,
-            lambda j, p: xb.at[(m, *plane(j), slice(None), slice(None), cut(p))],
-        )
+            lambda j, p: xb.at[(m, *plane(j), slice(None), slice(None), side_cut(0, p))],
+        )
+
+    def rows_second(m):
+        yield from gather(
+            wire, "z", NZ, z,
+            lambda j, p: xb.at[(m, *plane(j), k, slice(None), side_cut(HALF, p))],
+        )
+        mine = xb.at[m, :, :, k, :, pl.ds(HALF, HALF)]
+        moving = [wire(mine, mine, twin)]
+        yield
+        landed(moving)
 
     def whole_first():
         row = plane(z)
@@ -394,22 +400,45 @@
         across.append(pass_on(2, other))
         landed(across)
 
-    def sums_out(m):
+    summed = []
+
+    def products_of(m):
+        if m in summed:
+            return
+        summed.append(m)
         for core in (0, 1):
             part = jnp.zeros((NY * rows_of, 512), F32)
             for e in (0, 1):
                 rows = hb[m, e, :, core].reshape(NY * rows_of, WIDE)[:, :UNITS]
                 part = part + jnp.dot(rows, down_w[e, m], preferred_element_type=F32)
             yo[m, :, core] = part.astype(BF16).reshape(NY, PAIR, CAP, 512)
+
+    def out_first(m):
+        products_of(m)
         yield from scatter(
             wire, "z", NZ, z,
-            lambda j, p: yo.at[(m, *plane(j), slice(None), slice(None), cut(p))],
-            lambda n, p: za.at[m, n, :, :, cut(p)],
-        )
-        moving = [wire(yo.at[(m, *plane(z), 1 - k)], xa.at[m], twin)]
-        yield
-        landed(moving)
-        fin[m] = yo[(m, *plane(z), k)] + xa[m]
+            lambda j, p: yo.at[(m, *plane(j), slice(None), slice(None), side_cut(0, p))],
+            lambda n, p: za.at[m, n, :, :, side_cut(0, p)],
+        )
+        source = yo.at[(m, *plane(z), 1 - k, slice(None), pl.ds(0, HALF))]
+        moving = [wire(source, xa.at[m], twin)]
+        yield
+        landed(moving)
+        fin[m, :, 0:HALF] = yo[(m, *plane(z), k, slice(None), slice(0, HALF))] + xa[m]
+
+    def out_second(m):
+        products_of(m)
+        moving = [wire(yo.at[m, :, :, 1 - k, :, pl.ds(HALF, HALF)], xt.at[m], twin)]
+        yield
+        landed(moving)
+        right = slice(HALF, 2 * HALF)
+        yo[m, :, :, k, :, right] = yo[m, :, :, k, :, right] + xt[m]
+        yield from scatter(
+            wire, "z", NZ, z,
+            lambda j, p: yo.at[(m, *plane(j), k, slice(None), side_cut(HALF, p))],
+            lambda n, p: zt.at[m, n, :, side_cut(0, p)],
+        )
+        fin[m, :, right] = yo[(m, *plane(z), k, slice(None), right)]
 
     made = []
 
@@ -458,9 +487,10 @@
         )
         fin[WHOLE, :, HALF : 2 * HALF] = yf[(*plane(z), x, slice(None), slice(HALF, 2 * HALF))]
 
-    work = [rows_in(0), whole_first(), rows_in(2)]
+    work = [rows_first(0), whole_first(), rows_first(2)]
     work += [hidden(m, e) for m in range(MODS) for e in (0, 1)]
-    work += [sums_out(0), whole_out_first(), sums_out(2), whole_second(), whole_out_second()]
+    work += [out_first(0), whole_out_first(), out_first(2), whole_second(), whole_out_second()]
+    work += [rows_second(0), rows_second(2), out_second(0), out_second(2)]
     for n in ORDER:
         next(work[n], None)
     for process in work:
@@ -486,7 +516,7 @@
 
     greet(
         [{"x": around(x, o, NX)} for o in range(1, NX)]
-        + [{"z": around(z, o, NZ)} for o in range(1, NZ)]
+        + [{"z": around(z, o, NZ)} for o in (1, -1)]
         + [{"y": lax.div(p, 2), "c": lax.rem(p, 2)} for p in peers]
     )
     wire = Wire(send, recv)
@@ -561,8 +591,10 @@
         ((MODS, 2, 2, PAIR * CAP, 2 * WIDE), BF16),
         ((MODS, 2, NY, 2, PAIR * CAP, WIDE), BF16),
         ((MODS, NY, 2, PAIR, CAP, 512), BF16),
-        ((MODS, NZ, PAIR, CAP, 512), BF16),
-        ((MODS, CAP, 512), BF16),
+        ((MODS, NZ, PAIR, CAP, HALF), BF16),
+        ((MODS, CAP, HALF), BF16),
+        ((MODS, NZ, CAP, HALF), BF16),
+        ((MODS, NY, 2, CAP, HALF), BF16),
         ((NY, 2, NX, CAP, 512), BF16),
         ((NZ, NX, CAP, HALF), BF16),
         ((NX, CAP, HALF), BF16),
@@ -576,7 +608,7 @@
         out_shape=jax.ShapeDtypeStruct((ROWS, 512), BF16),
         in_specs=[pl.BlockSpec(memory_space=pl.ANY)] * 10,
         out_specs=pl.BlockSpec(memory_space=pltpu.VMEM),
-        scratch_shapes=[dma((280,)), dma((280,)), dma((12,))]
+        scratch_shapes=[dma((320,)), dma((320,)), dma((12,))]
         + [pltpu.VMEM(shape, kind) for shape, kind in shapes],
         compiler_params=pltpu.CompilerParams(
             collective_id=0, has_side_effects=True, vmem_limit_bytes=60 << 20

time: 152 us -> 147 us (0.967)
  Pallas kernels: 150 us -> 145 us
    pallas_call x1, Pallas kernels: 150 us -> 145 us  [on_device(): pl.pallas_call(layer_kernel, out_shape=jax.ShapeDtypeStruct((ROWS, 512),...]
where the time goes in v4:
time: 147 us
  Pallas kernels  145 us (99%)
  local copies, waits for them, and re-layouts  1.57 us (1%)
    pallas_call x1, Pallas kernels, on_device(): pl.pallas_call(layer_kernel, out_shape=jax.ShapeDtypeStruct((ROWS, 512),...  145 us

profile of v4, /device:TPU:2, one launch (start us, length us, event | category | flops | bytes accessed | tf_op | source)
XLA Modules:
  0.0 147.0 jit_solution(11574492535038051125)
XLA Ops:
  0.0 145.4 %layer.1 = bf16[128,512]{1,0:T(8,128)(2,1)} custom-call(bf16[128,512]{1,0:T(8,128)(2,1)} %args_0_.4, bf16[128,512]{1,0:T(8,128)(2,1)} %args_1_.4, bf16[128,512]{1,0:T(8,128)(2,1)} %args_2_.4, bf16[128,512]{1,0:T(8,128)(2,1)} %args_3_.4, s32[1,128]{1,0:T(1,128)} %bitcast.6, s32[1,128]{1,0:T(1,128)} %bitcast.7, f32[3,512]{1,0:T(4,128)} %args_6_.4, ...), custom_call_target="tpu_custom_call" | custom-call | tf_op jit(solution)/shard_map/layer/pallas_call | solution.py:606
  145.4 1.6 %copy.12 = bf16[128,512]{1,0:T(8,128)(2,1)} copy(bf16[128,512]{1,0:T(8,128)(2,1)} %layer.1) | data formatting | bytes 262144

commit v5 on v4

--- a/solution.py
+++ b/solution.py
@@ -109,6 +109,11 @@
         fetch(gain_ref, gain),
         fetch(resid_ref, resid),
     ]
+    greet(
+        [{"x": around(x, o, NX)} for o in range(1, NX)]
+        + [{"z": around(z, o, NZ)} for o in (1, -1)]
+        + [{"y": lax.div(p, 2), "c": lax.rem(p, 2)} for p in (around(t, o, 8) for o in range(1, 8))]
+    )
     sides = ((k_ref, kb, kr), (v_ref, vb, vr))
     coming, asked = {}, []
     for o in order[:3]:
@@ -218,7 +223,7 @@
     )
     stream[...] = flow
     sqb[t] = to_row(jnp.sum(flow * flow, axis=1, keepdims=True))
-    peers = [around(t, o, 8) for o in range(1, 8)]
+    peers = [around(t, o, 8) for o in (4, 3, 5, 2, 6, 1, 7)]
     coming = [wire(sqb.at[t], sqb.at[t], {"y": lax.div(p, 2), "c": lax.rem(p, 2)}) for p in peers]
     gains = jnp.where(
         tag_col == 0, gain[0:1, :], jnp.where(tag_col == 1, gain[1:2, :], gain[2:3, :])
@@ -505,7 +510,6 @@
     (xb, xf, stream, gate_w, up_w, down_w), args = args[:6], args[6:]
     attend_scratch, ffn_scratch = args[:16], args[16:]
     here = z, x, y, c = tuple(lax.axis_index(a) for a in ("z", "x", "y", "c"))
-    peers = [around(2 * y + c, o, 8) for o in range(1, 8)]
     fetched = []
 
     def fetch(src, dst):
@@ -514,11 +518,6 @@
         copy.start()
         return copy
 
-    greet(
-        [{"x": around(x, o, NX)} for o in range(1, NX)]
-        + [{"z": around(z, o, NZ)} for o in (1, -1)]
-        + [{"y": lax.div(p, 2), "c": lax.rem(p, 2)} for p in peers]
-    )
     wire = Wire(send, recv)
     tags, stream_ref, fin = attend_scratch[14], stream, ffn_scratch[-1]
     right, left = {"x": around(x, 1, NX)}, {"x": around(x, -1, NX)}

time: 147 us -> 147 us (level)
  no operation moved by 1% of the time
where the time goes in v5:
time: 147 us
  Pallas kernels  145 us (99%)
  local copies, waits for them, and re-layouts  1.57 us (1%)
    pallas_call x1, Pallas kernels, on_device(): pl.pallas_call(layer_kernel, out_shape=jax.ShapeDtypeStruct((ROWS, 512),...  145 us

profile of v5, /device:TPU:2, one launch (start us, length us, event | category | flops | bytes accessed | tf_op | source)
XLA Modules:
  0.0 147.0 jit_solution(3775343048327328276)
XLA Ops:
  0.0 145.4 %layer.1 = bf16[128,512]{1,0:T(8,128)(2,1)} custom-call(bf16[128,512]{1,0:T(8,128)(2,1)} %args_0_.4, bf16[128,512]{1,0:T(8,128)(2,1)} %args_1_.4, bf16[128,512]{1,0:T(8,128)(2,1)} %args_2_.4, bf16[128,512]{1,0:T(8,128)(2,1)} %args_3_.4, s32[1,128]{1,0:T(1,128)} %bitcast.6, s32[1,128]{1,0:T(1,128)} %bitcast.7, f32[3,512]{1,0:T(4,128)} %args_6_.4, ...), custom_call_target="tpu_custom_call" | custom-call | tf_op jit(solution)/shard_map/layer/pallas_call | solution.py:605
  145.5 1.6 %copy.12 = bf16[128,512]{1,0:T(8,128)(2,1)} copy(bf16[128,512]{1,0:T(8,128)(2,1)} %layer.1) | data formatting | bytes 262144
